TPU v7x, 32 devices: a whole 2x2x4 slice. The times are simulated.
32 devices in a mesh: clips: 2 (over y), tm: 4 (over x, core), rows: 4 (over z).
Axes of the slice: x: 2, y: 2, z: 4, core: 2. Of those that a mesh axis runs over, the one named last changes fastest.
Arguments:
- features: bfloat16 [8, 8, 48, 384], P(('clips', 'tm'), 'rows'), parts along dimension 0, may hold values from -320 to 320
- first_gain: float32 [384], replicated, may hold values from 0.5 to 1.5
- first_shift: float32 [384], replicated, may hold values from -3 to 3
- first_kernel: bfloat16 [384, 3, 3, 3, 384], P('tm'), may hold values from -0.0625 to 0.0625
- first_bias: float32 [384], P('tm'), may hold values from -2 to 2
- second_gain: float32 [384], replicated, may hold values from 0.5 to 1.5
- second_shift: float32 [384], replicated, may hold values from -3 to 3
- second_kernel: bfloat16 [384, 3, 3, 3, 384], P('tm'), may hold values from -0.0625 to 0.0625
- second_bias: float32 [384], P('tm'), may hold values from -2 to 2
- third_gain: float32 [384], replicated, may hold values from 0.5 to 1.5
- third_shift: float32 [384], replicated, may hold values from -3 to 3
- query_weight: bfloat16 [384, 384], replicated, may hold values from -0.30618622 to 0.30618622
- key_weight: bfloat16 [384, 384], replicated, may hold values from -1.8371173 to 1.8371173
- value_weight: bfloat16 [384, 384], replicated, may hold values from -0.3125 to 0.3125
- output_weight: bfloat16 [384, 384], replicated, may hold values from -0.3125 to 0.3125
Outputs:
- decoded: bfloat16 [8, 8, 48, 384], P(('clips', 'tm'), 'rows'), parts along dimension 0
There are 2 independent parts, one for each index of `clips`. A program takes and returns all parts, laid end to end along the dimension named above; an argument that names none is the same for every part. Nothing has to cross between parts.
All inputs are finite; a program needn't handle non-finite values.
Results may differ from a plain program's by a relative error of at most 0.029.
Values may be sent and summed in bfloat16 or wider, within the bound.
No kernel may reach another device: no remote copies, remote signals or barrier semaphores. Data moves between devices by JAX's collectives and lax.ppermute only.
A program may use at most 64 MiB of HBM per device.

v0:
```python
import functools

import jax
import jax.numpy as jnp
from jax import lax
from jax.experimental import pallas as pl
from jax.experimental.pallas import tpu as pltpu
from jax.sharding import PartitionSpec as P

C = 384
GROUPS = 32
GROUP = C // GROUPS
EPSILON = 1e-06
VMEM = pl.BlockSpec(memory_space=pltpu.VMEM)
SMEM = pl.BlockSpec(memory_space=pltpu.SMEM)
F32 = jnp.float32
BF16 = jnp.bfloat16


def call(body, outs, scratch=()):
    def run(*args):
        return pl.pallas_call(
            body,
            out_shape=outs,
            in_specs=[SMEM if a.dtype == jnp.int32 else VMEM for a in args],
            out_specs=jax.tree.map(lambda _: VMEM, outs),
            scratch_shapes=scratch,
            compiler_params=pltpu.CompilerParams(vmem_limit_bytes=16 * 1024 * 1024),
        )(*args)

    return run


def struct(shape, dtype=BF16):
    return jax.ShapeDtypeStruct(shape, dtype)


def group_sums(rows):
    channels = rows.shape[-1]
    first = lax.broadcasted_iota(jnp.int32, (channels, channels), 0)
    second = lax.broadcasted_iota(jnp.int32, (channels, channels), 1)
    same = ((first * 43691) >> 19) == ((second * 43691) >> 19)
    terms = jnp.concatenate(split3(rows), axis=0).astype(BF16)
    sums = jnp.dot(terms, same.astype(BF16), preferred_element_type=F32)
    size = rows.shape[0]
    return sums[0:size] + sums[size : 2 * size] + sums[2 * size :]


def split3(value):
    high = value.astype(BF16).astype(F32)
    rest = value - high
    middle = rest.astype(BF16).astype(F32)
    return high, middle, (rest - middle).astype(BF16).astype(F32)


def merge(means, squares, count):
    mean = sum(means) / len(means)
    spread = sum(jnp.square(m - mean) for m in means)
    return mean, (sum(squares) + count * spread) / (count * len(means))


def silu(value):
    return value / (1.0 + jnp.exp(-value))


def first_stats(r_ref, x_ref, near_ref, far_ref, own_ref, copy_ref):
    _, rows, cols, channels = x_ref.shape
    copy_ref[...] = x_ref[...]
    x = x_ref[0].astype(F32).reshape(rows * cols, channels)
    count = rows * cols * GROUP
    mean = group_sums(jnp.broadcast_to(jnp.sum(x, axis=0, keepdims=True), (8, channels)))[0:1] / count
    square = group_sums(
        jnp.broadcast_to(jnp.sum(jnp.square(x - mean), axis=0, keepdims=True), (8, channels))
    )[0:1]
    at = lax.broadcasted_iota(jnp.int32, (16, channels), 0)
    block = jnp.zeros((16, channels), F32)
    for i, term in enumerate(split3(mean) + split3(square)):
        block = jnp.where(at == i, term, block)
    block = block.astype(BF16)
    own_ref[...] = block
    odd = r_ref[0] & 1
    near_ref[0:cols] = x_ref[0, (rows - 1) * (1 - odd)]
    near_ref[cols : cols + 16] = block
    far_ref[0:cols] = x_ref[0, (rows - 1) * odd]
    far_ref[cols : cols + 16] = block


def load(w_ref, after_ref, out_ref, sem):
    copy = pltpu.make_async_copy(w_ref, out_ref, sem)
    copy.start()
    copy.wait()


def first_norm(n, r_ref, x_ref, near_ref, far_ref, own_ref, table_ref, loaded_ref, *refs):
    others, out_ref = refs[:-1], refs[-1]
    _, rows, cols, channels = x_ref.shape
    blocks = [own_ref[...].astype(F32)]
    if n == 4:
        far_block = far_ref[cols : cols + 16].astype(F32) + others[1][...].astype(F32)
        blocks += [near_ref[cols : cols + 16].astype(F32), far_block, others[0][...].astype(F32)]
    else:
        blocks = [others[0][i].astype(F32) for i in range(n)]
    means = [b[0:1] + b[1:2] + b[2:3] for b in blocks]
    squares = [b[3:4] + b[4:5] + b[5:6] for b in blocks]
    mean, variance = merge(means, squares, rows * cols * GROUP)
    scale = lax.rsqrt(variance + EPSILON) * table_ref[0:1]
    shift = table_ref[1:2]
    r = r_ref[0]

    def active(v):
        return silu((v.astype(F32) - mean) * scale + shift)

    odd = r & 1
    for row in range(rows):
        out_ref[0, 1 + row] = active(x_ref[0, row]).astype(BF16)
    out_ref[0, (1 + rows) * (1 - odd)] = active(near_ref[0:cols]).astype(BF16)
    beyond = jnp.logical_or(r == 0, r == n - 1)
    out_ref[0, (1 + rows) * odd] = jnp.where(beyond, 0.0, active(far_ref[0:cols])).astype(BF16)


def conv(a_ref, w_ref, bias):
    frames, padded, cols, channels = a_ref.shape
    rows = padded - 2
    outputs = w_ref.shape[2] // 3
    plane = rows * cols
    total = None
    for i in (2, 1, 0):
        count = frames - (2 - i)
        window = jnp.concatenate(
            [a_ref[0:count, j : j + rows].reshape(count * plane, channels) for j in range(3)], axis=1
        )
        weight = jnp.concatenate([w_ref[i, j] for j in range(3)], axis=1)
        term = lax.dot_general(window, weight, (((1,), (1,)), ((), ())), preferred_element_type=F32)
        if total is None:
            total = term
        else:
            head = (frames - count) * plane
            total = jnp.concatenate([total[:head], total[head:] + term], axis=0)
    col = lax.broadcasted_iota(jnp.int32, (frames * rows, cols, outputs), 1).reshape(frames * plane, outputs)
    left = pltpu.roll(total[:, 0:outputs], 1, 0)
    right = pltpu.roll(total[:, 2 * outputs :], frames * plane - 1, 0)
    result = total[:, outputs : 2 * outputs]
    result = result + jnp.where(col > 0, left, 0.0) + jnp.where(col < cols - 1, right, 0.0)
    return (result + bias).astype(BF16)


def first_conv(r_ref, a_ref, w_ref, bias_ref, out_ref, near_ref, far_ref, own_ref, rows8):
    frames, padded, cols, channels = a_ref.shape
    rows = padded - 2
    outputs = w_ref.shape[2] // 3
    plane = rows * cols
    result = conv(a_ref, w_ref, bias_ref[...].reshape(1, outputs))
    out_ref[...] = result.reshape(frames, rows, cols, outputs)
    wide = result.astype(F32).reshape(frames, plane, outputs)
    rows8[...] = jnp.zeros(rows8.shape, F32)
    for f in range(frames):
        rows8[f : f + 1] = jnp.sum(wide[f], axis=0, keepdims=True)
    mean = group_sums(rows8[...]) / (plane * GROUP)
    for f in range(frames):
        rows8[f : f + 1] = jnp.sum(jnp.square(wide[f] - mean[f : f + 1]), axis=0, keepdims=True)
    square = group_sums(rows8[...])
    block = jnp.concatenate(split3(mean) + split3(square), axis=0).astype(BF16)
    size = block.shape[0]
    own_ref[...] = block
    odd = r_ref[0] & 1
    for f in range(frames):
        near_ref[f * cols : (f + 1) * cols] = out_ref[f, (rows - 1) * (1 - odd)]
        far_ref[f * cols : (f + 1) * cols] = out_ref[f, (rows - 1) * odd]
    near_ref[frames * cols : frames * cols + size] = block
    far_ref[frames * cols : frames * cols + size] = block


def second_norm(n, r_ref, m_ref, x_ref, near_ref, far_ref, own_ref, table_ref, *refs):
    others, out_ref = refs[:-1], refs[-1]
    frames, rows, cols, channels = x_ref.shape
    gain, shift = (own_part(table_ref[i : i + 1], m_ref[0], channels) for i in (2, 3))
    step = 8 * (-(-frames // 8))
    size = 6 * step
    base = frames * cols
    blocks = [own_ref[...].astype(F32)]
    if n == 4:
        far_block = far_ref[base : base + size].astype(F32) + others[1][...].astype(F32)
        blocks += [near_ref[base : base + size].astype(F32), far_block, others[0][...].astype(F32)]
    else:
        blocks = [others[0][i].astype(F32) for i in range(n)]
    parts = [[b[q * step : (q + 1) * step] for q in range(6)] for b in blocks]
    means = [p[0] + p[1] + p[2] for p in parts]
    squares = [p[3] + p[4] + p[5] for p in parts]
    mean, variance = merge(means, squares, rows * cols * GROUP)
    scale = lax.rsqrt(variance + EPSILON) * gain
    r = r_ref[0]
    odd = r & 1
    beyond = jnp.logical_or(r == 0, r == n - 1)
    planes = []
    for f in range(frames):

        def active(v):
            return silu((v.astype(F32) - mean[f : f + 1]) * scale[f : f + 1] + shift)

        near = active(near_ref[f * cols : (f + 1) * cols])
        far = jnp.where(beyond, 0.0, active(far_ref[f * cols : (f + 1) * cols]))
        above, below = jnp.where(odd == 1, near, far), jnp.where(odd == 1, far, near)
        planes.append([above] + [active(x_ref[f, row]) for row in range(rows)] + [below])
    if packs(frames, channels):
        piece = channels // (frames - 1)
        for f in range(frames - 1):
            for row in range(rows + 2):
                extra = planes[-1][row][:, f * piece : (f + 1) * piece]
                out_ref[f, row] = jnp.concatenate([planes[f][row], extra], axis=1).astype(BF16)
    else:
        for f in range(frames):
            for row in range(rows + 2):
                out_ref[f, row] = planes[f][row].astype(BF16)


def packs(frames, channels):
    return channels % (frames - 1) == 0 and channels + channels // (frames - 1) == 128


def packed_shape(frames, rows, cols, channels):
    if packs(frames, channels):
        return (frames - 1, rows, cols, 128)
    return (frames, rows, cols, channels)


def own_part(row, which, size):
    result = row[:, 0:size]
    for i in range(1, row.shape[1] // size):
        result = jnp.where(which == i, row[:, i * size : (i + 1) * size], result)
    return result


def second_conv(m_ref, parts_ref, w_ref, bias_ref, *refs):
    outs, (a_ref, held) = refs[:-2], refs[-2:]
    count = parts_ref.shape[0]
    frames, padded, cols, channels = a_ref.shape
    part = channels // count
    for f in range(frames):
        for row in range(padded):
            if not packs(frames, part):
                pieces = [parts_ref[m, f, row] for m in range(count)]
            elif f < frames - 1:
                pieces = [parts_ref[m, f, row][:, 0:part] for m in range(count)]
            else:
                pieces = [parts_ref[m, g, row][:, part:] for m in range(count) for g in range(frames - 1)]
            a_ref[f, row] = jnp.concatenate(pieces, axis=1)
    result = conv(a_ref, w_ref, bias_ref[...].reshape(1, -1))
    held[...] = result.reshape(held.shape)
    for k, out_ref in enumerate(outs):
        out_ref[...] = held[m_ref[0] ^ k]


def add_hidden(m_ref, x_ref, *refs):
    parts, (out_ref, held) = refs[:-2], refs[-2:]
    _, rows, cols, channels = x_ref.shape
    for k, part in enumerate(parts):
        held[k] = part[...].astype(F32)
    update = jnp.concatenate([held[m_ref[0] ^ m] for m in range(len(parts))], axis=1)
    out_ref[...] = (x_ref[0].reshape(rows * cols, channels).astype(F32) + update).astype(BF16)


def attention(own_ref, *refs):
    others, (table_ref, wq_ref, wk_ref, wv_ref, wo_ref, out_ref) = refs[:-6], refs[-6:]
    channels = own_ref.shape[-1]
    gain, shift = table_ref[4:5], table_ref[5:6]
    own = own_ref[...].astype(F32)
    blocks = [o[...].reshape(-1, channels).astype(F32) for o in others]
    wide = blocks[0] if len(blocks) == 1 else jnp.concatenate([own] + blocks, axis=0)
    positions = wide.shape[0]
    count = positions * GROUP
    mean = group_sums(jnp.broadcast_to(jnp.sum(wide, axis=0, keepdims=True), (8, channels)))[0:1] / count
    centered = wide - mean
    variance = (
        group_sums(jnp.broadcast_to(jnp.sum(centered * centered, axis=0, keepdims=True), (8, channels)))[0:1]
        / count
    )
    scale = lax.rsqrt(variance + EPSILON) * gain
    normed = (centered * scale + shift).astype(BF16)
    mine = ((own - mean) * scale + shift).astype(BF16)
    dot = functools.partial(jnp.dot, preferred_element_type=F32)
    queries = (dot(mine, wq_ref[...]) * C ** (-0.5)).astype(BF16)
    keys = dot(normed, wk_ref[...]).astype(BF16)
    values = dot(normed, wv_ref[...]).astype(BF16)
    scores = lax.dot_general(queries, keys, (((1,), (1,)), ((), ())), preferred_element_type=F32)
    peak = jnp.max(scores, axis=-1, keepdims=True)
    weights = jnp.exp(scores - peak)
    total = jnp.sum(weights, axis=-1, keepdims=True)
    attended = (dot(weights.astype(BF16), values) / total).astype(BF16)
    out_ref[...] = (own + dot(attended, wo_ref[...])).astype(BF16)


def swapped(value, axis, partner, members=None):
    members = range(lax.axis_size(axis)) if members is None else members
    return lax.ppermute(value, axis, [(i, partner(i)) for i in members])


def around(near_message, far_message, own):
    n = lax.axis_size("rows")
    if n == 4:
        others = [swapped(own, "rows", lambda i: i ^ 2), swapped(own, "rows", lambda i: 3 - i, (0, 3))]
    else:
        others = [lax.all_gather(own, "rows")]
    return (
        swapped(near_message, "rows", lambda i: i ^ 1),
        swapped(far_message, "rows", lambda i: ((i + 1) ^ 1) - 1, range(1, n - 1)),
        others,
    )


def per_device(
    features,
    first_gain,
    first_shift,
    first_kernel,
    first_bias,
    second_gain,
    second_shift,
    second_kernel,
    second_bias,
    third_gain,
    third_shift,
    query_weight,
    key_weight,
    value_weight,
    output_weight,
):
    _, rows, cols, channels = features.shape
    n, frames = lax.axis_size("rows"), lax.axis_size("tm")
    outputs = first_kernel.shape[0]
    plane = rows * cols
    r = lax.axis_index("rows").astype(jnp.int32).reshape(1)
    m = lax.axis_index("tm").astype(jnp.int32).reshape(1)

    def taps(kernel):
        return jnp.transpose(kernel, (1, 2, 3, 0, 4)).reshape(3, 3, 3 * outputs, channels)

    message = struct((cols + 16, channels))
    row = lax.broadcasted_iota(jnp.int32, (8, channels), 0)
    table = jnp.zeros((8, channels), F32)
    for i, vector in enumerate([first_gain, first_shift, second_gain, second_shift, third_gain, third_shift]):
        table = jnp.where(row == i, vector[None, :], table)
    near_message, far_message, own, features = call(
        first_stats, (message, message, struct((16, channels)), struct(features.shape))
    )(r, features)
    near_message, far_message, others = around(near_message, far_message, own)
    weights1 = taps(first_kernel)
    weights1 = call(load, struct(weights1.shape), (pltpu.SemaphoreType.DMA,))(weights1, own)
    active1 = call(functools.partial(first_norm, n), struct((1, rows + 2, cols, channels)))(
        r, features, near_message, far_message, own, table, weights1, *others
    )
    clip = lax.all_gather(active1, "tm", axis=0, tiled=True)

    step = 8 * (-(-frames // 8))
    size = 6 * step
    message = struct((frames * cols + size, outputs))
    conv1, near_message, far_message, own = call(
        first_conv,
        (struct((frames, rows, cols, outputs)), message, message, struct((size, outputs))),
        (pltpu.VMEM((step, outputs), F32),),
    )(r, clip, weights1, first_bias)
    near_message, far_message, others = around(near_message, far_message, own)
    active2 = call(functools.partial(second_norm, n), struct(packed_shape(frames, rows + 2, cols, outputs)))(
        r, m, conv1, near_message, far_message, own, table, *others
    )
    parts = lax.all_gather(active2, "tm")
    piece = struct((plane, outputs))
    pieces = call(
        second_conv,
        [piece] * frames,
        (pltpu.VMEM((frames, rows + 2, cols, channels), BF16), pltpu.VMEM((frames, plane, outputs), BF16)),
    )(m, parts, taps(second_kernel), second_bias)
    pieces = [pieces[0]] + [swapped(pieces[k], "tm", lambda i, k=k: i ^ k) for k in range(1, frames)]
    hidden = call(add_hidden, struct((plane, channels)), (pltpu.VMEM((frames, plane, outputs), F32),))(
        m, features, *pieces
    )
    if n == 4:
        others = [swapped(hidden, "rows", lambda i, k=k: i ^ k) for k in (1, 2, 3)]
    else:
        others = [lax.all_gather(hidden, "rows")]
    decoded = call(attention, struct((plane, channels)))(
        hidden,
        *others,
        table,
        query_weight,
        key_weight,
        value_weight,
        output_weight,
    )
    return decoded.reshape(features.shape)


def solution(mesh):
    in_specs = (
        P(("clips", "tm"), "rows", None, None),
        P(),
        P(),
        P("tm", None, None, None, None),
        P("tm"),
        P(),
        P(),
        P("tm", None, None, None, None),
        P("tm"),
        P(),
        P(),
        P(),
        P(),
        P(),
        P(),
    )
    out_specs = P(("clips", "tm"), "rows", None, None)
    return jax.shard_map(
        per_device, mesh=mesh, in_specs=in_specs, out_specs=out_specs, check_vma=False
    )
```

profile of v0, /device:TPU:0, one launch (start us, length us, event | category | flops | bytes accessed | tf_op | source)
XLA Modules:
  0.0 61.3 jit_solution(2063244798176554277)
XLA Ops:
  0.0 0.9 %copy-done.6 = bf16[1,2,48,384]{3,2,1,0:T(8,128)(2,1)S(1)} copy-done((bf16[1,2,48,384]{3,2,1,0:T(8,128)(2,1)S(1)}, bf16[1,2,48,384]{3,2,1,0:T(8,128)(2,1)}, u32[]{:S(2)}) %copy-start.6) | copy-done | bytes 73752
  0.9 0.4 shard_map.145
  1.3 7.0 %collective-permute-start.3 = (bf16[16,384]{1,0:T(8,128)(2,1)S(1)}, bf16[16,384]{1,0:T(8,128)(2,1)S(1)}, u32[]{:S(2)}, u32[]{:S(2)}) collective-permute-start(bf16[16,384]{1,0:T(8,128)(2,1)S(1)} %get-tuple-element.20.after_ref.own_ref), channel_id=1, source_target_pairs={{0,3},{3,0},{4,7},{7,4},{8,11},{11,8},{12,15},{15,12},{16,19},{19,... | collective-permute-start | bytes 36872 | tf_op jit(solution)/shard_map/ppermute | solution.py:294
  8.3 0.1 collective-permute-start.2
  8.3 0.6 collective-permute-start
  8.9 0.7 %collective-permute-start.1 = (bf16[64,384]{1,0:T(8,128)(2,1)S(1)}, bf16[64,384]{1,0:T(8,128)(2,1)S(1)}, u32[]{:S(2)}, u32[]{:S(2)}) collective-permute-start(bf16[64,384]{1,0:T(8,128)(2,1)S(1)} %get-tuple-element.19), channel_id=1, source_target_pairs={{1,2},{2,1},{5,6},{6,5},{9,10},{10,9},{13,14},{14,13},{17,18},{18,... | collective-permute-start | bytes 147464 | tf_op jit(solution)/shard_map/ppermute | solution.py:294
  9.6 0.8 %select_select_fusion.table_ref.refs_3_ = f32[8,384]{1,0:T(8,128)S(1)} fusion(f32[384]{0:T(512)} %param.16, f32[384]{0:T(512)} %param.17, f32[384]{0:T(512)} %param.20, f32[384]{0:T(512)} %param.21, f32[384]{0:T(512)} %param.24, f32[384]{0:T(512)} %param.25, pred[8]{0:T(512)(128)(4,1)S(1)} %get-tuple-element.29, pred[8]{0:T(512)(128)(4,1)S(1)} %get-tuple-element.30, ...), kind=kLoop, calls=%fused_computation | loop fusion | flops 18432 | bytes 21552 | tf_op jit(solution)/shard_map/jit(_where)/select_n | solution.py:341
  10.4 1.5 %copy-done = bf16[96,3,3,3,384]{4,0,3,2,1:T(8,128)(2,1)S(1)} copy-done((bf16[96,3,3,3,384]{4,0,3,2,1:T(8,128)(2,1)S(1)}, bf16[96,3,3,3,384]{4,0,3,2,1:T(8,128)(2,1)}, u32[]{:S(2)}) %copy-start) | copy-done | bytes 1990680
  12.0 0.3 shard_map.146.loaded_ref.w_ref
  12.3 0.0 copy-start.7
  12.3 0.0 collective-permute-done.3.refs_1_
  12.4 0.6 collective-permute-done.2.refs_0_
  12.9 0.0 collective-permute-done.near_ref
  12.9 0.0 collective-permute-done.1.far_ref
  12.9 0.1 shard_map.147
  13.1 7.5 %all_gather.9.a_ref = bf16[4,4,48,384]{3,2,1,0:T(8,128)(2,1)S(1)} all-gather(bf16[1,4,48,384]{3,2,1,0:T(8,128)(2,1)S(1)} %shard_map.147), channel_id=1, replica_groups=mesh['clips'=2,'tm'=4,'rows'=4] {'tm'}, dimensions={0}, use_global_device_ids=true | all-gather | bytes 737280 | tf_op jit(solution)/shard_map/all_gather | solution.py:351
  20.6 0.0 copy-done.7
  20.6 2.0 %shard_map.148 = (bf16[4,2,48,96]{3,2,1,0:T(8,128)(2,1)S(1)}, bf16[240,96]{1,0:T(8,128)(2,1)S(1)}, bf16[240,96]{1,0:T(8,128)(2,1)S(1)}, bf16[48,96]{1,0:T(8,128)(2,1)S(1)}) custom-call(s32[1]{0:T(128)} %bitcast.1.r_ref, bf16[4,4,48,384]{3,2,1,0:T(8,128)(2,1)S(1)} %all_gather.9.a_ref, bf16[3,3,288,384]{3,2,1,0:T(8,128)(2,1)S(1)} %shard_map.146.loaded_ref.w_ref, ...), custom_call_target="tpu_custom_call" | custom-call | tf_op jit(solution)/shard_map/pallas_call | solution.py:22
  22.6 3.7 %collective-permute-start.4 = (bf16[240,96]{1,0:T(8,128)(2,1)S(1)}, bf16[240,96]{1,0:T(8,128)(2,1)S(1)}, u32[]{:S(2)}, u32[]{:S(2)}) collective-permute-start(bf16[240,96]{1,0:T(8,128)(2,1)S(1)} %get-tuple-element.22), channel_id=1, source_target_pairs={{0,1},{1,0},{2,3},{3,2},{4,5},{5,4},{6,7},{7,6},{8,9},{9,8},{10,11... | collective-permute-start | bytes 138248 | tf_op jit(solution)/shard_map/ppermute | solution.py:294
  26.3 0.7 %collective-permute-start.5 = (bf16[240,96]{1,0:T(8,128)(2,1)S(1)}, bf16[240,96]{1,0:T(8,128)(2,1)S(1)}, u32[]{:S(2)}, u32[]{:S(2)}) collective-permute-start(bf16[240,96]{1,0:T(8,128)(2,1)S(1)} %get-tuple-element.23), channel_id=1, source_target_pairs={{1,2},{2,1},{5,6},{6,5},{9,10},{10,9},{13,14},{14,13},{17,18},{18,... | collective-permute-start | bytes 138248 | tf_op jit(solution)/shard_map/ppermute | solution.py:294
  27.0 4.0 %collective-permute-start.7 = (bf16[48,96]{1,0:T(8,128)(2,1)S(1)}, bf16[48,96]{1,0:T(8,128)(2,1)S(1)}, u32[]{:S(2)}, u32[]{:S(2)}) collective-permute-start(bf16[48,96]{1,0:T(8,128)(2,1)S(1)} %get-tuple-element.24.own_ref), channel_id=1, source_target_pairs={{0,3},{3,0},{4,7},{7,4},{8,11},{11,8},{12,15},{15,12},{16,19},{19,... | collective-permute-start | bytes 27656 | tf_op jit(solution)/shard_map/ppermute | solution.py:294
  31.0 0.1 collective-permute-start.6
  31.1 3.3 %collective-permute-done.7.refs_1_ = bf16[48,96]{1,0:T(8,128)(2,1)S(1)} collective-permute-done((bf16[48,96]{1,0:T(8,128)(2,1)S(1)}, bf16[48,96]{1,0:T(8,128)(2,1)S(1)}, u32[]{:S(2)}, u32[]{:S(2)}) %collective-permute-start.7) | collective-permute-done | bytes 9248 | tf_op jit(solution)/shard_map/ppermute | solution.py:294
  34.4 1.3 %collective-permute-done.6.refs_0_ = bf16[48,96]{1,0:T(8,128)(2,1)S(1)} collective-permute-done((bf16[48,96]{1,0:T(8,128)(2,1)S(1)}, bf16[48,96]{1,0:T(8,128)(2,1)S(1)}, u32[]{:S(2)}, u32[]{:S(2)}) %collective-permute-start.6) | collective-permute-done | bytes 9248 | tf_op jit(solution)/shard_map/ppermute | solution.py:294
  35.7 0.0 collective-permute-done.4.near_ref
  35.7 0.0 collective-permute-done.5.far_ref
  35.7 0.0 copy-start.3
  35.7 0.0 copy-start.4
  35.7 0.0 copy-start.5
  35.8 0.3 shard_map.149
  36.1 6.7 %all-gather = bf16[12,4,48,128]{3,2,1,0:T(8,128)(2,1)S(1)} all-gather(bf16[3,4,48,128]{3,2,1,0:T(8,128)(2,1)S(1)} %shard_map.149), channel_id=2, replica_groups=mesh['clips'=2,'tm'=4,'rows'=4] {'tm'}, dimensions={0}, use_global_device_ids=true | all-gather | bytes 737280 | tf_op jit(solution)/shard_map/all_gather | solution.py:365
  42.8 0.0 copy-done.1
  42.8 1.6 %shard_map.150 = (bf16[96,96]{1,0:T(8,128)(2,1)S(1)}, bf16[96,96]{1,0:T(8,128)(2,1)S(1)}, bf16[96,96]{1,0:T(8,128)(2,1)S(1)}, bf16[96,96]{1,0:T(8,128)(2,1)S(1)}) custom-call(s32[1]{0:T(128)} %bitcast.m_ref, bf16[4,3,4,48,128]{4,3,2,1,0:T(8,128)(2,1)S(1)} %bitcast.10, bf16[3,3,288,384]{3,2,1,0:T(8,128)(2,1)S(1)} %bitcast.12, f32[96]{0:T(128)S(1)} %copy-done.8), custom_call_target="tpu_custom_call" | custom-call | tf_op jit(solution)/shard_map/pallas_call | solution.py:22
  44.4 0.4 collective-permute-start.8
  44.8 1.4 %collective-permute-start.9 = (bf16[96,96]{1,0:T(8,128)(2,1)S(1)}, bf16[96,96]{1,0:T(8,128)(2,1)S(1)}, u32[]{:S(2)}, u32[]{:S(2)}) collective-permute-start(bf16[96,96]{1,0:T(8,128)(2,1)S(1)} %get-tuple-element.27), channel_id=1, source_target_pairs={{0,8},{4,12},{8,0},{12,4},{1,9},{5,13},{9,1},{13,5},{2,10},{6,14},... | collective-permute-start | bytes 55304 | tf_op jit(solution)/shard_map/ppermute | solution.py:294
  46.2 0.1 collective-permute-start.10
  46.3 0.0 collective-permute-done.8.refs_1_
  46.3 2.3 %collective-permute-done.9.refs_2_ = bf16[96,96]{1,0:T(8,128)(2,1)S(1)} collective-permute-done((bf16[96,96]{1,0:T(8,128)(2,1)S(1)}, bf16[96,96]{1,0:T(8,128)(2,1)S(1)}, u32[]{:S(2)}, u32[]{:S(2)}) %collective-permute-start.9) | collective-permute-done | bytes 18464 | tf_op jit(solution)/shard_map/ppermute | solution.py:294
  48.6 1.0 %collective-permute-done.10.refs_3_ = bf16[96,96]{1,0:T(8,128)(2,1)S(1)} collective-permute-done((bf16[96,96]{1,0:T(8,128)(2,1)S(1)}, bf16[96,96]{1,0:T(8,128)(2,1)S(1)}, u32[]{:S(2)}, u32[]{:S(2)}) %collective-permute-start.10) | collective-permute-done | bytes 18464 | tf_op jit(solution)/shard_map/ppermute | solution.py:294
  49.6 0.1 shard_map.151.own_ref
  49.8 1.8 %collective-permute-start.13 = (bf16[96,384]{1,0:T(8,128)(2,1)S(1)}, bf16[96,384]{1,0:T(8,128)(2,1)S(1)}, u32[]{:S(2)}, u32[]{:S(2)}) collective-permute-start(bf16[96,384]{1,0:T(8,128)(2,1)S(1)} %shard_map.151.own_ref), channel_id=1, source_target_pairs={{0,3},{1,2},{2,1},{3,0},{4,7},{5,6},{6,5},{7,4},{8,11},{9,10},{10,... | collective-permute-start | bytes 221192 | tf_op jit(solution)/shard_map/ppermute | solution.py:294
  51.5 0.0 collective-permute-start.12
  51.5 2.7 %collective-permute-start.11 = (bf16[96,384]{1,0:T(8,128)(2,1)S(1)}, bf16[96,384]{1,0:T(8,128)(2,1)S(1)}, u32[]{:S(2)}, u32[]{:S(2)}) collective-permute-start(bf16[96,384]{1,0:T(8,128)(2,1)S(1)} %shard_map.151.own_ref), channel_id=1, source_target_pairs={{0,1},{1,0},{2,3},{3,2},{4,5},{5,4},{6,7},{7,6},{8,9},{9,8},{10,11... | collective-permute-start | bytes 221192 | tf_op jit(solution)/shard_map/ppermute | solution.py:294
  54.2 2.6 %collective-permute-done.13.refs_2_ = bf16[96,384]{1,0:T(8,128)(2,1)S(1)} collective-permute-done((bf16[96,384]{1,0:T(8,128)(2,1)S(1)}, bf16[96,384]{1,0:T(8,128)(2,1)S(1)}, u32[]{:S(2)}, u32[]{:S(2)}) %collective-permute-start.13) | collective-permute-done | bytes 73760 | tf_op jit(solution)/shard_map/ppermute | solution.py:294
  56.8 2.3 %collective-permute-done.12.refs_1_ = bf16[96,384]{1,0:T(8,128)(2,1)S(1)} collective-permute-done((bf16[96,384]{1,0:T(8,128)(2,1)S(1)}, bf16[96,384]{1,0:T(8,128)(2,1)S(1)}, u32[]{:S(2)}, u32[]{:S(2)}) %collective-permute-start.12) | collective-permute-done | bytes 73760 | tf_op jit(solution)/shard_map/ppermute | solution.py:294
  59.1 0.0 collective-permute-done.11.refs_0_
  59.1 0.0 copy-done.2
  59.1 2.2 %shard_map.152 = bf16[96,384]{1,0:T(8,128)(2,1)} custom-call(bf16[96,384]{1,0:T(8,128)(2,1)S(1)} %shard_map.151.own_ref, bf16[96,384]{1,0:T(8,128)(2,1)S(1)} %collective-permute-done.11.refs_0_, bf16[96,384]{1,0:T(8,128)(2,1)S(1)} %collective-permute-done.12.refs_1_, bf16[96,384]{1,0:T(8,128)(2,1)S(1)} %collective-permute-done.13.refs_2_, ...), custom_call_target="tpu_custom_call" | custom-call | tf_op jit(solution)/shard_map/pallas_call | solution.py:22
  (12 shorter events, 0.0 us)
Async XLA Ops:
  0.0 0.9 %copy-start.6 = (bf16[1,2,48,384]{3,2,1,0:T(8,128)(2,1)S(1)}, bf16[1,2,48,384]{3,2,1,0:T(8,128)(2,1)}, u32[]{:S(2)}) copy-start(bf16[1,2,48,384]{3,2,1,0:T(8,128)(2,1)} %x_ref.1) | copy-start | bytes 221188
  1.3 11.1 %collective-permute-start.3 = (bf16[16,384]{1,0:T(8,128)(2,1)S(1)}, bf16[16,384]{1,0:T(8,128)(2,1)S(1)}, u32[]{:S(2)}, u32[]{:S(2)}) collective-permute-start(bf16[16,384]{1,0:T(8,128)(2,1)S(1)} %get-tuple-element.20.after_ref.own_ref), channel_id=1, source_target_pairs={{0,3},{3,0},{4,7},{7,4},{8,11},{11,8},{12,15},{15,12},{16,19},{19,... | collective-permute-start | bytes 36872 | tf_op jit(solution)/shard_map/ppermute | solution.py:294
  8.3 4.7 %collective-permute-start.2 = (bf16[16,384]{1,0:T(8,128)(2,1)S(1)}, bf16[16,384]{1,0:T(8,128)(2,1)S(1)}, u32[]{:S(2)}, u32[]{:S(2)}) collective-permute-start(bf16[16,384]{1,0:T(8,128)(2,1)S(1)} %get-tuple-element.20.after_ref.own_ref), channel_id=1, source_target_pairs={{0,2},{1,3},{2,0},{3,1},{4,6},{5,7},{6,4},{7,5},{8,10},{9,11},{10,... | collective-permute-start | bytes 36872 | tf_op jit(solution)/shard_map/ppermute | solution.py:294
  8.3 4.6 %collective-permute-start = (bf16[64,384]{1,0:T(8,128)(2,1)S(1)}, bf16[64,384]{1,0:T(8,128)(2,1)S(1)}, u32[]{:S(2)}, u32[]{:S(2)}) collective-permute-start(bf16[64,384]{1,0:T(8,128)(2,1)S(1)} %get-tuple-element.18), channel_id=1, source_target_pairs={{0,1},{1,0},{2,3},{3,2},{4,5},{5,4},{6,7},{7,6},{8,9},{9,8},{10,11... | collective-permute-start | bytes 147464 | tf_op jit(solution)/shard_map/ppermute | solution.py:294
  8.9 4.0 %collective-permute-start.1 = (bf16[64,384]{1,0:T(8,128)(2,1)S(1)}, bf16[64,384]{1,0:T(8,128)(2,1)S(1)}, u32[]{:S(2)}, u32[]{:S(2)}) collective-permute-start(bf16[64,384]{1,0:T(8,128)(2,1)S(1)} %get-tuple-element.19), channel_id=1, source_target_pairs={{1,2},{2,1},{5,6},{6,5},{9,10},{10,9},{13,14},{14,13},{17,18},{18,... | collective-permute-start | bytes 147464 | tf_op jit(solution)/shard_map/ppermute | solution.py:294
  10.4 1.6 %copy-start = (bf16[96,3,3,3,384]{4,0,3,2,1:T(8,128)(2,1)S(1)}, bf16[96,3,3,3,384]{4,0,3,2,1:T(8,128)(2,1)}, u32[]{:S(2)}) copy-start(bf16[96,3,3,3,384]{4,0,3,2,1:T(8,128)(2,1)} %param.18) | copy-start | bytes 5971972
  12.3 8.3 %copy-start.7 = (f32[96]{0:T(128)S(1)}, f32[96]{0:T(128)}, u32[]{:S(2)}) copy-start(f32[96]{0:T(128)} %bias_ref.2) | copy-start | bytes 1156
  20.6 22.2 %copy-start.1 = (bf16[96,3,3,3,384]{4,0,3,2,1:T(8,128)(2,1)S(1)}, bf16[96,3,3,3,384]{4,0,3,2,1:T(8,128)(2,1)}, u32[]{:S(2)}) copy-start(bf16[96,3,3,3,384]{4,0,3,2,1:T(8,128)(2,1)} %param.22) | copy-start | bytes 5971972
  20.6 22.2 %copy-start.8 = (f32[96]{0:T(128)S(1)}, f32[96]{0:T(128)}, u32[]{:S(2)}) copy-start(f32[96]{0:T(128)} %bias_ref.3) | copy-start | bytes 1156
  22.6 13.1 %collective-permute-start.4 = (bf16[240,96]{1,0:T(8,128)(2,1)S(1)}, bf16[240,96]{1,0:T(8,128)(2,1)S(1)}, u32[]{:S(2)}, u32[]{:S(2)}) collective-permute-start(bf16[240,96]{1,0:T(8,128)(2,1)S(1)} %get-tuple-element.22), channel_id=1, source_target_pairs={{0,1},{1,0},{2,3},{3,2},{4,5},{5,4},{6,7},{7,6},{8,9},{9,8},{10,11... | collective-permute-start | bytes 138248 | tf_op jit(solution)/shard_map/ppermute | solution.py:294
  26.3 9.4 %collective-permute-start.5 = (bf16[240,96]{1,0:T(8,128)(2,1)S(1)}, bf16[240,96]{1,0:T(8,128)(2,1)S(1)}, u32[]{:S(2)}, u32[]{:S(2)}) collective-permute-start(bf16[240,96]{1,0:T(8,128)(2,1)S(1)} %get-tuple-element.23), channel_id=1, source_target_pairs={{1,2},{2,1},{5,6},{6,5},{9,10},{10,9},{13,14},{14,13},{17,18},{18,... | collective-permute-start | bytes 138248 | tf_op jit(solution)/shard_map/ppermute | solution.py:294
  27.0 7.4 %collective-permute-start.7 = (bf16[48,96]{1,0:T(8,128)(2,1)S(1)}, bf16[48,96]{1,0:T(8,128)(2,1)S(1)}, u32[]{:S(2)}, u32[]{:S(2)}) collective-permute-start(bf16[48,96]{1,0:T(8,128)(2,1)S(1)} %get-tuple-element.24.own_ref), channel_id=1, source_target_pairs={{0,3},{3,0},{4,7},{7,4},{8,11},{11,8},{12,15},{15,12},{16,19},{19,... | collective-permute-start | bytes 27656 | tf_op jit(solution)/shard_map/ppermute | solution.py:294
  31.0 4.7 %collective-permute-start.6 = (bf16[48,96]{1,0:T(8,128)(2,1)S(1)}, bf16[48,96]{1,0:T(8,128)(2,1)S(1)}, u32[]{:S(2)}, u32[]{:S(2)}) collective-permute-start(bf16[48,96]{1,0:T(8,128)(2,1)S(1)} %get-tuple-element.24.own_ref), channel_id=1, source_target_pairs={{0,2},{1,3},{2,0},{3,1},{4,6},{5,7},{6,4},{7,5},{8,10},{9,11},{10,... | collective-permute-start | bytes 27656 | tf_op jit(solution)/shard_map/ppermute | solution.py:294
  35.7 23.4 %copy-start.2 = (bf16[384,384]{1,0:T(8,128)(2,1)S(1)}, bf16[384,384]{1,0:T(8,128)(2,1)}, u32[]{:S(2)}) copy-start(bf16[384,384]{1,0:T(8,128)(2,1)} %refs_4_.1) | copy-start | bytes 884740
  35.7 23.4 %copy-start.3 = (bf16[384,384]{1,0:T(8,128)(2,1)S(1)}, bf16[384,384]{1,0:T(8,128)(2,1)}, u32[]{:S(2)}) copy-start(bf16[384,384]{1,0:T(8,128)(2,1)} %refs_5_.1) | copy-start | bytes 884740
  35.7 23.4 %copy-start.4 = (bf16[384,384]{1,0:T(8,128)(2,1)S(1)}, bf16[384,384]{1,0:T(8,128)(2,1)}, u32[]{:S(2)}) copy-start(bf16[384,384]{1,0:T(8,128)(2,1)} %refs_6_.1) | copy-start | bytes 884740
  35.7 23.4 %copy-start.5 = (bf16[384,384]{1,0:T(8,128)(2,1)S(1)}, bf16[384,384]{1,0:T(8,128)(2,1)}, u32[]{:S(2)}) copy-start(bf16[384,384]{1,0:T(8,128)(2,1)} %refs_7_.1) | copy-start | bytes 884740
  44.4 1.9 %collective-permute-start.8 = (bf16[96,96]{1,0:T(8,128)(2,1)S(1)}, bf16[96,96]{1,0:T(8,128)(2,1)S(1)}, u32[]{:S(2)}, u32[]{:S(2)}) collective-permute-start(bf16[96,96]{1,0:T(8,128)(2,1)S(1)} %get-tuple-element.26), channel_id=1, source_target_pairs={{0,4},{4,0},{8,12},{12,8},{1,5},{5,1},{9,13},{13,9},{2,6},{6,2},{1... | collective-permute-start | bytes 55304 | tf_op jit(solution)/shard_map/ppermute | solution.py:294
  44.8 3.8 %collective-permute-start.9 = (bf16[96,96]{1,0:T(8,128)(2,1)S(1)}, bf16[96,96]{1,0:T(8,128)(2,1)S(1)}, u32[]{:S(2)}, u32[]{:S(2)}) collective-permute-start(bf16[96,96]{1,0:T(8,128)(2,1)S(1)} %get-tuple-element.27), channel_id=1, source_target_pairs={{0,8},{4,12},{8,0},{12,4},{1,9},{5,13},{9,1},{13,5},{2,10},{6,14},... | collective-permute-start | bytes 55304 | tf_op jit(solution)/shard_map/ppermute | solution.py:294
  46.2 3.5 %collective-permute-start.10 = (bf16[96,96]{1,0:T(8,128)(2,1)S(1)}, bf16[96,96]{1,0:T(8,128)(2,1)S(1)}, u32[]{:S(2)}, u32[]{:S(2)}) collective-permute-start(bf16[96,96]{1,0:T(8,128)(2,1)S(1)} %get-tuple-element.28), channel_id=1, source_target_pairs={{0,12},{4,8},{8,4},{12,0},{1,13},{5,9},{9,5},{13,1},{2,14},{6,10},... | collective-permute-start | bytes 55304 | tf_op jit(solution)/shard_map/ppermute | solution.py:294
  49.8 7.0 %collective-permute-start.13 = (bf16[96,384]{1,0:T(8,128)(2,1)S(1)}, bf16[96,384]{1,0:T(8,128)(2,1)S(1)}, u32[]{:S(2)}, u32[]{:S(2)}) collective-permute-start(bf16[96,384]{1,0:T(8,128)(2,1)S(1)} %shard_map.151.own_ref), channel_id=1, source_target_pairs={{0,3},{1,2},{2,1},{3,0},{4,7},{5,6},{6,5},{7,4},{8,11},{9,10},{10,... | collective-permute-start | bytes 221192 | tf_op jit(solution)/shard_map/ppermute | solution.py:294
  51.5 7.6 %collective-permute-start.12 = (bf16[96,384]{1,0:T(8,128)(2,1)S(1)}, bf16[96,384]{1,0:T(8,128)(2,1)S(1)}, u32[]{:S(2)}, u32[]{:S(2)}) collective-permute-start(bf16[96,384]{1,0:T(8,128)(2,1)S(1)} %shard_map.151.own_ref), channel_id=1, source_target_pairs={{0,2},{1,3},{2,0},{3,1},{4,6},{5,7},{6,4},{7,5},{8,10},{9,11},{10,... | collective-permute-start | bytes 221192 | tf_op jit(solution)/shard_map/ppermute | solution.py:294
  51.5 7.6 %collective-permute-start.11 = (bf16[96,384]{1,0:T(8,128)(2,1)S(1)}, bf16[96,384]{1,0:T(8,128)(2,1)S(1)}, u32[]{:S(2)}, u32[]{:S(2)}) collective-permute-start(bf16[96,384]{1,0:T(8,128)(2,1)S(1)} %shard_map.151.own_ref), channel_id=1, source_target_pairs={{0,1},{1,0},{2,3},{3,2},{4,5},{5,4},{6,7},{7,6},{8,9},{9,8},{10,11... | collective-permute-start | bytes 221192 | tf_op jit(solution)/shard_map/ppermute | solution.py:294
where the time goes:
time: 61.6 us; the launch traced here: 61.3 us
  starting transfers between devices  23.1 us (38%)
  blocking collectives  14.2 us (23%)
  waiting for transfers between devices  13.3 us (22%)
  Pallas kernels  7.14 us (12%)
  local copies, waits for them, and re-layouts  2.47 us (4%)
  other arithmetic  0.86 us (1%)
    ppermute x14, starting transfers between devices, swapped(): return lax.ppermute(value, axis, [(i, partner(i)) for i in members])  23.1 us
    ppermute x14, waiting for transfers between devices, swapped(): return lax.ppermute(value, axis, [(i, partner(i)) for i in members])  13.3 us
    all_gather x1, blocking collectives, per_device(): clip = lax.all_gather(active1, 'tm', axis=0, tiled=True)  7.53 us
    pallas_call x8, Pallas kernels, run(): pl.pallas_call(body, out_shape=outs, in_specs=[SMEM if a.dtype == jnp.int...  7.14 us
    all_gather x1, blocking collectives, per_device(): parts = lax.all_gather(active2, 'tm')  6.69 us
    unnamed x18, local copies, waits for them, and re-layouts  2.47 us
  transfers between devices with their start and end apart: 14, of which 7 were waited for; matrix products, arithmetic and copies ran while one was open for 1% of the time, Pallas kernels for 1%

commit v1 on v0

--- a/solution.py
+++ b/solution.py
@@ -96,8 +96,8 @@
     _, rows, cols, channels = x_ref.shape
     blocks = [own_ref[...].astype(F32)]
     if n == 4:
-        far_block = far_ref[cols : cols + 16].astype(F32) + others[1][...].astype(F32)
-        blocks += [near_ref[cols : cols + 16].astype(F32), far_block, others[0][...].astype(F32)]
+        blocks += [near_ref[cols : cols + 16].astype(F32), far_ref[cols : cols + 16].astype(F32)]
+        blocks += [others[0][...].astype(F32)]
     else:
         blocks = [others[0][i].astype(F32) for i in range(n)]
     means = [b[0:1] + b[1:2] + b[2:3] for b in blocks]
@@ -118,38 +118,75 @@
     out_ref[0, (1 + rows) * odd] = jnp.where(beyond, 0.0, active(far_ref[0:cols])).astype(BF16)
 
 
-def conv(a_ref, w_ref, bias):
-    frames, padded, cols, channels = a_ref.shape
+def add_taps(total_ref, a_ref, w_ref, lanes, first, last):
+    _, padded, cols, channels = a_ref.shape
     rows = padded - 2
-    outputs = w_ref.shape[2] // 3
     plane = rows * cols
-    total = None
+    frames = total_ref.shape[0] // plane
     for i in (2, 1, 0):
-        count = frames - (2 - i)
+        count = min(last, frames - (2 - i)) - first
+        if count <= 0:
+            continue
         window = jnp.concatenate(
             [a_ref[0:count, j : j + rows].reshape(count * plane, channels) for j in range(3)], axis=1
         )
-        weight = jnp.concatenate([w_ref[i, j] for j in range(3)], axis=1)
-        term = lax.dot_general(window, weight, (((1,), (1,)), ((), ())), preferred_element_type=F32)
-        if total is None:
-            total = term
-        else:
-            head = (frames - count) * plane
-            total = jnp.concatenate([total[:head], total[head:] + term], axis=0)
-    col = lax.broadcasted_iota(jnp.int32, (frames * rows, cols, outputs), 1).reshape(frames * plane, outputs)
-    left = pltpu.roll(total[:, 0:outputs], 1, 0)
-    right = pltpu.roll(total[:, 2 * outputs :], frames * plane - 1, 0)
-    result = total[:, outputs : 2 * outputs]
+        weight = jnp.concatenate([w_ref[i, j, :, lanes] for j in range(3)], axis=1)
+        start = (first + 2 - i) * plane
+        total_ref[start : start + count * plane] += lax.dot_general(
+            window, weight, (((1,), (1,)), ((), ())), preferred_element_type=F32
+        )
+
+
+def finish(total_ref, cols, bias_ref):
+    positions = total_ref.shape[0]
+    outputs = total_ref.shape[1] // 3
+    col = lax.broadcasted_iota(jnp.int32, (positions // cols, cols, outputs), 1).reshape(positions, outputs)
+    left = pltpu.roll(total_ref[:, 0:outputs], 1, 0)
+    right = pltpu.roll(total_ref[:, 2 * outputs :], positions - 1, 0)
+    result = total_ref[:, outputs : 2 * outputs]
     result = result + jnp.where(col > 0, left, 0.0) + jnp.where(col < cols - 1, right, 0.0)
-    return (result + bias).astype(BF16)
-
-
-def first_conv(r_ref, a_ref, w_ref, bias_ref, out_ref, near_ref, far_ref, own_ref, rows8):
-    frames, padded, cols, channels = a_ref.shape
-    rows = padded - 2
-    outputs = w_ref.shape[2] // 3
+    return (result + bias_ref[...].reshape(1, outputs)).astype(BF16)
+
+
+def on_half(m_ref, other, body):
+    half = m_ref[0] >> 1
+    for h in (0, 1):
+        pl.when(half == (1 - h if other else h))(functools.partial(body, h))
+
+
+def hand_on(x_ref, after_ref, out_ref):
+    out_ref[...] = x_ref[...]
+
+
+def first_conv_near(m_ref, own_ref, mate_ref, w_ref, total_ref, pair):
+    odd = m_ref[0] & 1
+    pair[odd] = own_ref[0]
+    pair[1 - odd] = mate_ref[0]
+    total_ref[...] = jnp.zeros(total_ref.shape, F32)
+    on_half(m_ref, False, lambda h: add_taps(total_ref, pair, w_ref, slice(None), 2 * h, 2 * h + 2))
+
+
+def first_conv_rest(r_ref, m_ref, near_total_ref, own_ref, mate_ref, w_ref, bias_ref, *refs):
+    outs, (pair, total, rows8) = refs[:-3], refs[-3:]
+    odd = m_ref[0] & 1
+    pair[odd] = own_ref[0]
+    pair[1 - odd] = mate_ref[0]
+    total[...] = near_total_ref[...]
+    on_half(m_ref, True, lambda h: add_taps(total, pair, w_ref, slice(None), 2 * h, 2 * h + 2))
+    first_finish(r_ref, total, bias_ref, *outs, rows8)
+
+
+def first_conv(r_ref, a_ref, w_ref, bias_ref, *refs):
+    outs, (total, rows8) = refs[:-2], refs[-2:]
+    total[...] = jnp.zeros(total.shape, F32)
+    add_taps(total, a_ref, w_ref, slice(None), 0, a_ref.shape[0])
+    first_finish(r_ref, total, bias_ref, *outs, rows8)
+
+
+def first_finish(r_ref, total_ref, bias_ref, out_ref, near_ref, far_ref, own_ref, rows8):
+    frames, rows, cols, outputs = out_ref.shape
     plane = rows * cols
-    result = conv(a_ref, w_ref, bias_ref[...].reshape(1, outputs))
+    result = finish(total_ref, cols, bias_ref)
     out_ref[...] = result.reshape(frames, rows, cols, outputs)
     wide = result.astype(F32).reshape(frames, plane, outputs)
     rows8[...] = jnp.zeros(rows8.shape, F32)
@@ -179,8 +216,8 @@
     base = frames * cols
     blocks = [own_ref[...].astype(F32)]
     if n == 4:
-        far_block = far_ref[base : base + size].astype(F32) + others[1][...].astype(F32)
-        blocks += [near_ref[base : base + size].astype(F32), far_block, others[0][...].astype(F32)]
+        blocks += [near_ref[base : base + size].astype(F32), far_ref[base : base + size].astype(F32)]
+        blocks += [others[0][...].astype(F32)]
     else:
         blocks = [others[0][i].astype(F32) for i in range(n)]
     parts = [[b[q * step : (q + 1) * step] for q in range(6)] for b in blocks]
@@ -230,22 +267,63 @@
     return result
 
 
+def unpack(part_ref, f, row, part, frames):
+    if not packs(frames, part):
+        return part_ref[f, row]
+    if f < frames - 1:
+        return part_ref[f, row][:, 0:part]
+    return jnp.concatenate([part_ref[g, row][:, part:] for g in range(frames - 1)], axis=1)
+
+
+def pair_taps(h, total_ref, even_ref, odd_ref, w_ref, a_ref):
+    frames, padded, cols, lanes = a_ref.shape
+    channels = w_ref.shape[3]
+    part = channels // 4
+    fill = jnp.zeros((cols, lanes - 2 * part), BF16)
+    for f in range(frames):
+        for row in range(padded):
+            pieces = [unpack(ref, f, row, part, frames) for ref in (even_ref, odd_ref)]
+            a_ref[f, row] = jnp.concatenate([fill] + pieces if h else pieces + [fill], axis=1)
+    where = slice(channels - lanes, channels) if h else slice(0, lanes)
+    add_taps(total_ref, a_ref, w_ref, where, 0, frames)
+
+
+def in_order(m_ref, own_ref, mate_ref, both):
+    odd = m_ref[0] & 1
+    both[odd] = own_ref[...]
+    both[1 - odd] = mate_ref[...]
+    return both.at[0], both.at[1]
+
+
+def second_conv_near(m_ref, own_ref, mate_ref, w_ref, total_ref, both, a_ref):
+    even, odd = in_order(m_ref, own_ref, mate_ref, both)
+    total_ref[...] = jnp.zeros(total_ref.shape, F32)
+    on_half(m_ref, False, lambda h: pair_taps(h, total_ref, even, odd, w_ref, a_ref))
+
+
+def second_conv_rest(m_ref, near_total_ref, own_ref, mate_ref, w_ref, bias_ref, *refs):
+    outs, (both, a_ref, total, held) = refs[:-4], refs[-4:]
+    even, odd = in_order(m_ref, own_ref, mate_ref, both)
+    total[...] = near_total_ref[...]
+    on_half(m_ref, True, lambda h: pair_taps(h, total, even, odd, w_ref, a_ref))
+    second_finish(m_ref, total, a_ref.shape[2], bias_ref, outs, held)
+
+
 def second_conv(m_ref, parts_ref, w_ref, bias_ref, *refs):
-    outs, (a_ref, held) = refs[:-2], refs[-2:]
+    outs, (a_ref, total, held) = refs[:-3], refs[-3:]
     count = parts_ref.shape[0]
     frames, padded, cols, channels = a_ref.shape
-    part = channels // count
     for f in range(frames):
         for row in range(padded):
-            if not packs(frames, part):
-                pieces = [parts_ref[m, f, row] for m in range(count)]
-            elif f < frames - 1:
-                pieces = [parts_ref[m, f, row][:, 0:part] for m in range(count)]
-            else:
-                pieces = [parts_ref[m, g, row][:, part:] for m in range(count) for g in range(frames - 1)]
+            pieces = [unpack(parts_ref.at[m], f, row, channels // count, frames) for m in range(count)]
             a_ref[f, row] = jnp.concatenate(pieces, axis=1)
-    result = conv(a_ref, w_ref, bias_ref[...].reshape(1, -1))
-    held[...] = result.reshape(held.shape)
+    total[...] = jnp.zeros(total.shape, F32)
+    add_taps(total, a_ref, w_ref, slice(None), 0, frames)
+    second_finish(m_ref, total, cols, bias_ref, outs, held)
+
+
+def second_finish(m_ref, total_ref, cols, bias_ref, outs, held):
+    held[...] = finish(total_ref, cols, bias_ref).reshape(held.shape)
     for k, out_ref in enumerate(outs):
         out_ref[...] = held[m_ref[0] ^ k]
 
@@ -289,20 +367,23 @@
     out_ref[...] = (own + dot(attended, wo_ref[...])).astype(BF16)
 
 
-def swapped(value, axis, partner, members=None):
-    members = range(lax.axis_size(axis)) if members is None else members
-    return lax.ppermute(value, axis, [(i, partner(i)) for i in members])
+def swapped(value, axis, partner):
+    return lax.ppermute(value, axis, [(i, partner(i)) for i in range(lax.axis_size(axis))])
+
+
+def far(i, n):
+    return ((i + 1) ^ 1) - 1 if 0 < i < n - 1 else n - 1 - i
 
 
 def around(near_message, far_message, own):
     n = lax.axis_size("rows")
     if n == 4:
-        others = [swapped(own, "rows", lambda i: i ^ 2), swapped(own, "rows", lambda i: 3 - i, (0, 3))]
+        others = [swapped(own, "rows", lambda i: i ^ 2)]
     else:
         others = [lax.all_gather(own, "rows")]
     return (
         swapped(near_message, "rows", lambda i: i ^ 1),
-        swapped(far_message, "rows", lambda i: ((i + 1) ^ 1) - 1, range(1, n - 1)),
+        swapped(far_message, "rows", functools.partial(far, n=n)),
         others,
     )
 
@@ -348,27 +429,51 @@
     active1 = call(functools.partial(first_norm, n), struct((1, rows + 2, cols, channels)))(
         r, features, near_message, far_message, own, table, weights1, *others
     )
-    clip = lax.all_gather(active1, "tm", axis=0, tiled=True)
 
     step = 8 * (-(-frames // 8))
     size = 6 * step
     message = struct((frames * cols + size, outputs))
-    conv1, near_message, far_message, own = call(
-        first_conv,
-        (struct((frames, rows, cols, outputs)), message, message, struct((size, outputs))),
-        (pltpu.VMEM((step, outputs), F32),),
-    )(r, clip, weights1, first_bias)
+    conv1_outs = (struct((frames, rows, cols, outputs)), message, message, struct((size, outputs)))
+    total = struct((frames * plane, 3 * outputs), F32)
+    total_scratch = pltpu.VMEM(total.shape, F32)
+    stats_scratch = pltpu.VMEM((step, outputs), F32)
+    bias1, bias2 = first_bias, second_bias
+    split = frames == 4 and channels == 4 * outputs and 2 * outputs <= 256 < channels
+    if split:
+        pair = pltpu.VMEM((2, rows + 2, cols, channels), BF16)
+        across = swapped(active1, "tm", lambda i: i ^ 2)
+        mate = swapped(active1, "tm", lambda i: i ^ 1)
+        near_total = call(first_conv_near, total, (pair,))(m, active1, mate, weights1)
+        beside = swapped(call(hand_on, struct(across.shape))(across, near_total), "tm", lambda i: i ^ 1)
+        conv1, near_message, far_message, own = call(
+            first_conv_rest, conv1_outs, (pair, total_scratch, stats_scratch)
+        )(r, m, near_total, across, beside, weights1, bias1)
+    else:
+        clip = lax.all_gather(active1, "tm", axis=0, tiled=True)
+        conv1, near_message, far_message, own = call(first_conv, conv1_outs, (total_scratch, stats_scratch))(
+            r, clip, weights1, bias1
+        )
     near_message, far_message, others = around(near_message, far_message, own)
     active2 = call(functools.partial(second_norm, n), struct(packed_shape(frames, rows + 2, cols, outputs)))(
         r, m, conv1, near_message, far_message, own, table, *others
     )
-    parts = lax.all_gather(active2, "tm")
     piece = struct((plane, outputs))
-    pieces = call(
-        second_conv,
-        [piece] * frames,
-        (pltpu.VMEM((frames, rows + 2, cols, channels), BF16), pltpu.VMEM((frames, plane, outputs), BF16)),
-    )(m, parts, taps(second_kernel), second_bias)
+    held = pltpu.VMEM((frames, plane, outputs), BF16)
+    weights2 = taps(second_kernel)
+    if split:
+        both = pltpu.VMEM((2, *active2.shape), BF16)
+        half = pltpu.VMEM((frames, rows + 2, cols, 256), BF16)
+        across = swapped(active2, "tm", lambda i: i ^ 2)
+        mate = swapped(active2, "tm", lambda i: i ^ 1)
+        near_total = call(second_conv_near, total, (both, half))(m, active2, mate, weights2)
+        beside = swapped(call(hand_on, struct(across.shape))(across, near_total), "tm", lambda i: i ^ 1)
+        pieces = call(second_conv_rest, [piece] * frames, (both, half, total_scratch, held))(
+            m, near_total, across, beside, weights2, bias2
+        )
+    else:
+        parts = lax.all_gather(active2, "tm")
+        whole = pltpu.VMEM((frames, rows + 2, cols, channels), BF16)
+        pieces = call(second_conv, [piece] * frames, (whole, total_scratch, held))(m, parts, weights2, bias2)
     pieces = [pieces[0]] + [swapped(pieces[k], "tm", lambda i, k=k: i ^ k) for k in range(1, frames)]
     hidden = call(add_hidden, struct((plane, channels)), (pltpu.VMEM((frames, plane, outputs), F32),))(
         m, features, *pieces

time: 61.6 us -> 56.3 us (0.914)
  blocking collectives: 14.2 us -> 0 us
  waiting for transfers between devices: 13.3 us -> 24.5 us
  starting transfers between devices: 23.1 us -> 19.4 us
  Pallas kernels: 7.14 us -> 8.65 us
    all_gather x2 -> x0, blocking collectives: 14.2 us -> none  [the longest x1 7.53 us: per_device(): clip = lax.all_gather(active1, 'tm', axis=0, tiled=True)]
    ppermute x14 -> x18, waiting for transfers between devices: 13.3 us -> 24.5 us  [swapped(): lax.ppermute(value, axis, [(i, partner(i)) for i in range(lax.axis_size(a...]
    ppermute x14 -> x18, starting transfers between devices: 23.1 us -> 19.4 us  [swapped(): lax.ppermute(value, axis, [(i, partner(i)) for i in range(lax.axis_size(a...]
    pallas_call x8 -> x12, Pallas kernels: 7.14 us -> 8.65 us  [run(): pl.pallas_call(body, out_shape=outs, in_specs=[SMEM if a.dtype == jnp.int...]
  transfers between devices with their start and end apart: 14 -> 18, of which waited for: 7 -> 10; matrix products, arithmetic and copies ran while one was open for 1% -> 2% of each run, Pallas kernels for 1% -> 4%
where the time goes in v1:
time: 56.3 us; the launch traced here: 56 us
  waiting for transfers between devices  24.5 us (44%)
  starting transfers between devices  19.4 us (34%)
  Pallas kernels  8.65 us (15%)
  local copies, waits for them, and re-layouts  2.47 us (4%)
  other arithmetic  0.86 us (2%)
    ppermute x18, waiting for transfers between devices, swapped(): lax.ppermute(value, axis, [(i, partner(i)) for i in range(lax.axis_size(a...  24.5 us
    ppermute x18, starting transfers between devices, swapped(): lax.ppermute(value, axis, [(i, partner(i)) for i in range(lax.axis_size(a...  19.4 us
    pallas_call x12, Pallas kernels, run(): pl.pallas_call(body, out_shape=outs, in_specs=[SMEM if a.dtype == jnp.int...  8.65 us
    unnamed x18, local copies, waits for them, and re-layouts  2.47 us
  transfers between devices with their start and end apart: 18, of which 10 were waited for; matrix products, arithmetic and copies ran while one was open for 2% of the time, Pallas kernels for 4%

profile of v1, /device:TPU:0, one launch (start us, length us, event | category | flops | bytes accessed | tf_op | source)
XLA Modules:
  0.0 56.0 jit_solution(11423160164275066648)
XLA Ops:
  0.0 0.9 %copy-done.6 = bf16[1,2,48,384]{3,2,1,0:T(8,128)(2,1)S(1)} copy-done((bf16[1,2,48,384]{3,2,1,0:T(8,128)(2,1)S(1)}, bf16[1,2,48,384]{3,2,1,0:T(8,128)(2,1)}, u32[]{:S(2)}) %copy-start.6) | copy-done | bytes 73752
  0.9 0.4 shard_map.145
  1.3 4.1 %collective-permute-start.2 = (bf16[16,384]{1,0:T(8,128)(2,1)S(1)}, bf16[16,384]{1,0:T(8,128)(2,1)S(1)}, u32[]{:S(2)}, u32[]{:S(2)}) collective-permute-start(bf16[16,384]{1,0:T(8,128)(2,1)S(1)} %get-tuple-element.20.after_ref.own_ref), channel_id=1, source_target_pairs={{0,2},{1,3},{2,0},{3,1},{4,6},{5,7},{6,4},{7,5},{8,10},{9,11},{10,... | collective-permute-start | bytes 36872 | tf_op jit(solution)/shard_map/ppermute | solution.py:371
  5.4 1.6 %collective-permute-start = (bf16[64,384]{1,0:T(8,128)(2,1)S(1)}, bf16[64,384]{1,0:T(8,128)(2,1)S(1)}, u32[]{:S(2)}, u32[]{:S(2)}) collective-permute-start(bf16[64,384]{1,0:T(8,128)(2,1)S(1)} %get-tuple-element.18), channel_id=1, source_target_pairs={{0,1},{1,0},{2,3},{3,2},{4,5},{5,4},{6,7},{7,6},{8,9},{9,8},{10,11... | collective-permute-start | bytes 147464 | tf_op jit(solution)/shard_map/ppermute | solution.py:371
  7.0 0.8 %select_select_fusion.table_ref.refs_3_ = f32[8,384]{1,0:T(8,128)S(1)} fusion(f32[384]{0:T(512)} %param.16, f32[384]{0:T(512)} %param.17, f32[384]{0:T(512)} %param.20, f32[384]{0:T(512)} %param.21, f32[384]{0:T(512)} %param.24, f32[384]{0:T(512)} %param.25, pred[8]{0:T(512)(128)(4,1)S(1)} %get-tuple-element.29, pred[8]{0:T(512)(128)(4,1)S(1)} %get-tuple-element.30, ...), kind=kLoop, calls=%fused_computation | loop fusion | flops 18432 | bytes 21552 | tf_op jit(solution)/shard_map/jit(_where)/select_n | solution.py:422
  7.9 1.5 %copy-done.1 = bf16[96,3,3,3,384]{4,0,3,2,1:T(8,128)(2,1)S(1)} copy-done((bf16[96,3,3,3,384]{4,0,3,2,1:T(8,128)(2,1)S(1)}, bf16[96,3,3,3,384]{4,0,3,2,1:T(8,128)(2,1)}, u32[]{:S(2)}) %copy-start.1) | copy-done | bytes 1990680
  9.4 0.3 shard_map.146.loaded_ref.w_ref
  9.7 0.0 collective-permute-done.2.refs_0_
  9.7 0.0 collective-permute-done.near_ref
  9.8 3.1 %collective-permute-done.1.far_ref = bf16[64,384]{1,0:T(8,128)(2,1)S(1)} collective-permute-done((bf16[64,384]{1,0:T(8,128)(2,1)S(1)}, bf16[64,384]{1,0:T(8,128)(2,1)S(1)}, u32[]{:S(2)}, u32[]{:S(2)}) %collective-permute-start.1) | collective-permute-done | bytes 49184 | tf_op jit(solution)/shard_map/ppermute | solution.py:371
  12.9 0.1 shard_map.147.own_ref
  13.0 0.0 copy-start.7
  13.0 0.1 collective-permute-start.3
  13.1 1.6 %collective-permute-start.4 = (bf16[1,4,48,384]{3,2,1,0:T(8,128)(2,1)S(1)}, bf16[1,4,48,384]{3,2,1,0:T(8,128)(2,1)S(1)}, u32[]{:S(2)}, u32[]{:S(2)}) collective-permute-start(bf16[1,4,48,384]{3,2,1,0:T(8,128)(2,1)S(1)} %shard_map.147.own_ref), channel_id=1, source_target_pairs={{0,8},{4,12},{8,0},{12,4},{1,9},{5,13},{9,1},{13,5},{2,10},{6,14},... | collective-permute-start | bytes 442376 | tf_op jit(solution)/shard_map/ppermute | solution.py:371
  14.6 1.1 %shard_map.148.after_ref.near_total_ref = f32[384,288]{1,0:T(8,128)S(1)} custom-call(s32[1]{0:T(128)} %bitcast.m_ref, bf16[1,4,48,384]{3,2,1,0:T(8,128)(2,1)S(1)} %shard_map.147.own_ref, bf16[1,4,48,384]{3,2,1,0:T(8,128)(2,1)S(1)} %collective-permute-done.3.mate_ref, bf16[3,3,288,384]{3,2,1,0:T(8,128)(2,1)S(1)} %shard_map.146.loaded_ref.w_ref), custom_call_target="tpu_custom_call" | custom-call | tf_op jit(solution)/shard_map/pallas_call | solution.py:22
  15.7 0.0 copy-start
  15.7 3.6 %collective-permute-done.4.x_ref.own_ref = bf16[1,4,48,384]{3,2,1,0:T(8,128)(2,1)S(1)} collective-permute-done((bf16[1,4,48,384]{3,2,1,0:T(8,128)(2,1)S(1)}, bf16[1,4,48,384]{3,2,1,0:T(8,128)(2,1)S(1)}, u32[]{:S(2)}, u32[]{:S(2)}) %collective-permute-start.4) | collective-permute-done | bytes 147488 | tf_op jit(solution)/shard_map/ppermute | solution.py:371
  19.4 0.1 collective-permute-start.5
  19.4 1.4 %collective-permute-done.5.mate_ref = bf16[1,4,48,384]{3,2,1,0:T(8,128)(2,1)S(1)} collective-permute-done((bf16[1,4,48,384]{3,2,1,0:T(8,128)(2,1)S(1)}, bf16[1,4,48,384]{3,2,1,0:T(8,128)(2,1)S(1)}, u32[]{:S(2)}, u32[]{:S(2)}) %collective-permute-start.5) | collective-permute-done | bytes 147488 | tf_op jit(solution)/shard_map/ppermute | solution.py:371
  20.8 1.5 %shard_map.150 = (bf16[4,2,48,96]{3,2,1,0:T(8,128)(2,1)S(1)}, bf16[240,96]{1,0:T(8,128)(2,1)S(1)}, bf16[240,96]{1,0:T(8,128)(2,1)S(1)}, bf16[48,96]{1,0:T(8,128)(2,1)S(1)}) custom-call(s32[1]{0:T(128)} %bitcast.1.r_ref, s32[1]{0:T(128)} %bitcast.m_ref, f32[384,288]{1,0:T(8,128)S(1)} %shard_map.148.after_ref.near_total_ref, ...), custom_call_target="tpu_custom_call" | custom-call | tf_op jit(solution)/shard_map/pallas_call | solution.py:22
  22.4 0.1 collective-permute-start.6
  22.4 0.8 %collective-permute-start.7 = (bf16[240,96]{1,0:T(8,128)(2,1)S(1)}, bf16[240,96]{1,0:T(8,128)(2,1)S(1)}, u32[]{:S(2)}, u32[]{:S(2)}) collective-permute-start(bf16[240,96]{1,0:T(8,128)(2,1)S(1)} %get-tuple-element.23), channel_id=1, source_target_pairs={{0,3},{1,2},{2,1},{3,0},{4,7},{5,6},{6,5},{7,4},{8,11},{9,10},{10,... | collective-permute-start | bytes 138248 | tf_op jit(solution)/shard_map/ppermute | solution.py:371
  23.2 2.7 %collective-permute-start.8 = (bf16[48,96]{1,0:T(8,128)(2,1)S(1)}, bf16[48,96]{1,0:T(8,128)(2,1)S(1)}, u32[]{:S(2)}, u32[]{:S(2)}) collective-permute-start(bf16[48,96]{1,0:T(8,128)(2,1)S(1)} %get-tuple-element.24.own_ref), channel_id=1, source_target_pairs={{0,2},{1,3},{2,0},{3,1},{4,6},{5,7},{6,4},{7,5},{8,10},{9,11},{10,... | collective-permute-start | bytes 27656 | tf_op jit(solution)/shard_map/ppermute | solution.py:371
  25.9 3.6 %collective-permute-done.8.refs_0_ = bf16[48,96]{1,0:T(8,128)(2,1)S(1)} collective-permute-done((bf16[48,96]{1,0:T(8,128)(2,1)S(1)}, bf16[48,96]{1,0:T(8,128)(2,1)S(1)}, u32[]{:S(2)}, u32[]{:S(2)}) %collective-permute-start.8) | collective-permute-done | bytes 9248 | tf_op jit(solution)/shard_map/ppermute | solution.py:371
  29.5 0.3 shard_map.151.own_ref
  29.8 0.1 collective-permute-start.9
  29.9 1.9 %collective-permute-start.10 = (bf16[3,4,48,128]{3,2,1,0:T(8,128)(2,1)S(1)}, bf16[3,4,48,128]{3,2,1,0:T(8,128)(2,1)S(1)}, u32[]{:S(2)}, u32[]{:S(2)}) collective-permute-start(bf16[3,4,48,128]{3,2,1,0:T(8,128)(2,1)S(1)} %shard_map.151.own_ref), channel_id=1, source_target_pairs={{0,8},{4,12},{8,0},{12,4},{1,9},{5,13},{9,1},{13,5},{2,10},{6,14},... | collective-permute-start | bytes 442376 | tf_op jit(solution)/shard_map/ppermute | solution.py:371
  31.8 1.0 %shard_map.152.after_ref.near_total_ref = f32[384,288]{1,0:T(8,128)S(1)} custom-call(s32[1]{0:T(128)} %bitcast.m_ref, bf16[3,4,48,128]{3,2,1,0:T(8,128)(2,1)S(1)} %shard_map.151.own_ref, bf16[3,4,48,128]{3,2,1,0:T(8,128)(2,1)S(1)} %collective-permute-done.9.mate_ref, bf16[3,3,288,384]{3,2,1,0:T(8,128)(2,1)S(1)} %bitcast.9), custom_call_target="tpu_custom_call" | custom-call | tf_op jit(solution)/shard_map/pallas_call | solution.py:22
  32.9 0.0 copy-start.2
  32.9 0.0 copy-start.3
  32.9 0.0 copy-start.4
  32.9 0.0 copy-start.5
  32.9 3.3 %collective-permute-done.10.x_ref.own_ref = bf16[3,4,48,128]{3,2,1,0:T(8,128)(2,1)S(1)} collective-permute-done((bf16[3,4,48,128]{3,2,1,0:T(8,128)(2,1)S(1)}, bf16[3,4,48,128]{3,2,1,0:T(8,128)(2,1)S(1)}, u32[]{:S(2)}, u32[]{:S(2)}) %collective-permute-start.10) | collective-permute-done | bytes 147488 | tf_op jit(solution)/shard_map/ppermute | solution.py:371
  36.3 0.1 collective-permute-start.11
  36.3 1.4 %collective-permute-done.11.mate_ref = bf16[3,4,48,128]{3,2,1,0:T(8,128)(2,1)S(1)} collective-permute-done((bf16[3,4,48,128]{3,2,1,0:T(8,128)(2,1)S(1)}, bf16[3,4,48,128]{3,2,1,0:T(8,128)(2,1)S(1)}, u32[]{:S(2)}, u32[]{:S(2)}) %collective-permute-start.11) | collective-permute-done | bytes 147488 | tf_op jit(solution)/shard_map/ppermute | solution.py:371
  37.7 1.5 %shard_map.154 = (bf16[96,96]{1,0:T(8,128)(2,1)S(1)}, bf16[96,96]{1,0:T(8,128)(2,1)S(1)}, bf16[96,96]{1,0:T(8,128)(2,1)S(1)}, bf16[96,96]{1,0:T(8,128)(2,1)S(1)}) custom-call(s32[1]{0:T(128)} %bitcast.m_ref, f32[384,288]{1,0:T(8,128)S(1)} %shard_map.152.after_ref.near_total_ref, bf16[3,4,48,128]{3,2,1,0:T(8,128)(2,1)S(1)} %collective-permute-done.10.x_ref.own_ref, ...), custom_call_target="tpu_custom_call" | custom-call | tf_op jit(solution)/shard_map/pallas_call | solution.py:22
  39.2 0.2 collective-permute-start.12
  39.4 1.7 %collective-permute-start.13 = (bf16[96,96]{1,0:T(8,128)(2,1)S(1)}, bf16[96,96]{1,0:T(8,128)(2,1)S(1)}, u32[]{:S(2)}, u32[]{:S(2)}) collective-permute-start(bf16[96,96]{1,0:T(8,128)(2,1)S(1)} %get-tuple-element.27), channel_id=1, source_target_pairs={{0,8},{4,12},{8,0},{12,4},{1,9},{5,13},{9,1},{13,5},{2,10},{6,14},... | collective-permute-start | bytes 55304 | tf_op jit(solution)/shard_map/ppermute | solution.py:371
  41.1 0.0 collective-permute-start.14
  41.2 2.1 %collective-permute-done.13.refs_2_ = bf16[96,96]{1,0:T(8,128)(2,1)S(1)} collective-permute-done((bf16[96,96]{1,0:T(8,128)(2,1)S(1)}, bf16[96,96]{1,0:T(8,128)(2,1)S(1)}, u32[]{:S(2)}, u32[]{:S(2)}) %collective-permute-start.13) | collective-permute-done | bytes 18464 | tf_op jit(solution)/shard_map/ppermute | solution.py:371
  43.3 1.1 %collective-permute-done.14.refs_3_ = bf16[96,96]{1,0:T(8,128)(2,1)S(1)} collective-permute-done((bf16[96,96]{1,0:T(8,128)(2,1)S(1)}, bf16[96,96]{1,0:T(8,128)(2,1)S(1)}, u32[]{:S(2)}, u32[]{:S(2)}) %collective-permute-start.14) | collective-permute-done | bytes 18464 | tf_op jit(solution)/shard_map/ppermute | solution.py:371
  44.4 0.1 shard_map.155.own_ref
  44.5 1.5 %collective-permute-start.17 = (bf16[96,384]{1,0:T(8,128)(2,1)S(1)}, bf16[96,384]{1,0:T(8,128)(2,1)S(1)}, u32[]{:S(2)}, u32[]{:S(2)}) collective-permute-start(bf16[96,384]{1,0:T(8,128)(2,1)S(1)} %shard_map.155.own_ref), channel_id=1, source_target_pairs={{0,3},{1,2},{2,1},{3,0},{4,7},{5,6},{6,5},{7,4},{8,11},{9,10},{10,... | collective-permute-start | bytes 221192 | tf_op jit(solution)/shard_map/ppermute | solution.py:371
  46.0 0.5 collective-permute-start.16
  46.5 2.5 %collective-permute-start.15 = (bf16[96,384]{1,0:T(8,128)(2,1)S(1)}, bf16[96,384]{1,0:T(8,128)(2,1)S(1)}, u32[]{:S(2)}, u32[]{:S(2)}) collective-permute-start(bf16[96,384]{1,0:T(8,128)(2,1)S(1)} %shard_map.155.own_ref), channel_id=1, source_target_pairs={{0,1},{1,0},{2,3},{3,2},{4,5},{5,4},{6,7},{7,6},{8,9},{9,8},{10,11... | collective-permute-start | bytes 221192 | tf_op jit(solution)/shard_map/ppermute | solution.py:371
  49.0 2.6 %collective-permute-done.17.refs_2_ = bf16[96,384]{1,0:T(8,128)(2,1)S(1)} collective-permute-done((bf16[96,384]{1,0:T(8,128)(2,1)S(1)}, bf16[96,384]{1,0:T(8,128)(2,1)S(1)}, u32[]{:S(2)}, u32[]{:S(2)}) %collective-permute-start.17) | collective-permute-done | bytes 73760 | tf_op jit(solution)/shard_map/ppermute | solution.py:371
  51.6 2.3 %collective-permute-done.16.refs_1_ = bf16[96,384]{1,0:T(8,128)(2,1)S(1)} collective-permute-done((bf16[96,384]{1,0:T(8,128)(2,1)S(1)}, bf16[96,384]{1,0:T(8,128)(2,1)S(1)}, u32[]{:S(2)}, u32[]{:S(2)}) %collective-permute-start.16) | collective-permute-done | bytes 73760 | tf_op jit(solution)/shard_map/ppermute | solution.py:371
  53.9 2.2 %shard_map.156 = bf16[96,384]{1,0:T(8,128)(2,1)} custom-call(bf16[96,384]{1,0:T(8,128)(2,1)S(1)} %shard_map.155.own_ref, bf16[96,384]{1,0:T(8,128)(2,1)S(1)} %collective-permute-done.15.refs_0_, bf16[96,384]{1,0:T(8,128)(2,1)S(1)} %collective-permute-done.16.refs_1_, bf16[96,384]{1,0:T(8,128)(2,1)S(1)} %collective-permute-done.17.refs_2_, ...), custom_call_target="tpu_custom_call" | custom-call | tf_op jit(solution)/shard_map/pallas_call | solution.py:22
  (22 shorter events, 0.1 us)
Async XLA Ops:
  0.0 0.9 %copy-start.6 = (bf16[1,2,48,384]{3,2,1,0:T(8,128)(2,1)S(1)}, bf16[1,2,48,384]{3,2,1,0:T(8,128)(2,1)}, u32[]{:S(2)}) copy-start(bf16[1,2,48,384]{3,2,1,0:T(8,128)(2,1)} %x_ref.1) | copy-start | bytes 221188
  1.3 8.4 %collective-permute-start.2 = (bf16[16,384]{1,0:T(8,128)(2,1)S(1)}, bf16[16,384]{1,0:T(8,128)(2,1)S(1)}, u32[]{:S(2)}, u32[]{:S(2)}) collective-permute-start(bf16[16,384]{1,0:T(8,128)(2,1)S(1)} %get-tuple-element.20.after_ref.own_ref), channel_id=1, source_target_pairs={{0,2},{1,3},{2,0},{3,1},{4,6},{5,7},{6,4},{7,5},{8,10},{9,11},{10,... | collective-permute-start | bytes 36872 | tf_op jit(solution)/shard_map/ppermute | solution.py:371
  5.4 4.4 %collective-permute-start = (bf16[64,384]{1,0:T(8,128)(2,1)S(1)}, bf16[64,384]{1,0:T(8,128)(2,1)S(1)}, u32[]{:S(2)}, u32[]{:S(2)}) collective-permute-start(bf16[64,384]{1,0:T(8,128)(2,1)S(1)} %get-tuple-element.18), channel_id=1, source_target_pairs={{0,1},{1,0},{2,3},{3,2},{4,5},{5,4},{6,7},{7,6},{8,9},{9,8},{10,11... | collective-permute-start | bytes 147464 | tf_op jit(solution)/shard_map/ppermute | solution.py:371
  7.0 5.9 %collective-permute-start.1 = (bf16[64,384]{1,0:T(8,128)(2,1)S(1)}, bf16[64,384]{1,0:T(8,128)(2,1)S(1)}, u32[]{:S(2)}, u32[]{:S(2)}) collective-permute-start(bf16[64,384]{1,0:T(8,128)(2,1)S(1)} %get-tuple-element.19), channel_id=1, source_target_pairs={{0,3},{1,2},{2,1},{3,0},{4,7},{5,6},{6,5},{7,4},{8,11},{9,10},{10,... | collective-permute-start | bytes 147464 | tf_op jit(solution)/shard_map/ppermute | solution.py:371
  7.8 1.6 %copy-start.1 = (bf16[96,3,3,3,384]{4,0,3,2,1:T(8,128)(2,1)S(1)}, bf16[96,3,3,3,384]{4,0,3,2,1:T(8,128)(2,1)}, u32[]{:S(2)}) copy-start(bf16[96,3,3,3,384]{4,0,3,2,1:T(8,128)(2,1)} %param.18) | copy-start | bytes 5971972
  13.0 7.8 %copy-start.7 = (f32[96]{0:T(128)S(1)}, f32[96]{0:T(128)}, u32[]{:S(2)}) copy-start(f32[96]{0:T(128)} %bias_ref.2) | copy-start | bytes 1156
  13.0 1.6 %collective-permute-start.3 = (bf16[1,4,48,384]{3,2,1,0:T(8,128)(2,1)S(1)}, bf16[1,4,48,384]{3,2,1,0:T(8,128)(2,1)S(1)}, u32[]{:S(2)}, u32[]{:S(2)}) collective-permute-start(bf16[1,4,48,384]{3,2,1,0:T(8,128)(2,1)S(1)} %shard_map.147.own_ref), channel_id=1, source_target_pairs={{0,4},{4,0},{8,12},{12,8},{1,5},{5,1},{9,13},{13,9},{2,6},{6,2},{1... | collective-permute-start | bytes 442376 | tf_op jit(solution)/shard_map/ppermute | solution.py:371
  13.1 6.3 %collective-permute-start.4 = (bf16[1,4,48,384]{3,2,1,0:T(8,128)(2,1)S(1)}, bf16[1,4,48,384]{3,2,1,0:T(8,128)(2,1)S(1)}, u32[]{:S(2)}, u32[]{:S(2)}) collective-permute-start(bf16[1,4,48,384]{3,2,1,0:T(8,128)(2,1)S(1)} %shard_map.147.own_ref), channel_id=1, source_target_pairs={{0,8},{4,12},{8,0},{12,4},{1,9},{5,13},{9,1},{13,5},{2,10},{6,14},... | collective-permute-start | bytes 442376 | tf_op jit(solution)/shard_map/ppermute | solution.py:371
  15.7 16.1 %copy-start = (bf16[96,3,3,3,384]{4,0,3,2,1:T(8,128)(2,1)S(1)}, bf16[96,3,3,3,384]{4,0,3,2,1:T(8,128)(2,1)}, u32[]{:S(2)}) copy-start(bf16[96,3,3,3,384]{4,0,3,2,1:T(8,128)(2,1)} %param.22) | copy-start | bytes 5971972
  19.4 1.4 %collective-permute-start.5 = (bf16[1,4,48,384]{3,2,1,0:T(8,128)(2,1)S(1)}, bf16[1,4,48,384]{3,2,1,0:T(8,128)(2,1)S(1)}, u32[]{:S(2)}, u32[]{:S(2)}) collective-permute-start(bf16[1,4,48,384]{3,2,1,0:T(8,128)(2,1)S(1)} %shard_map.149), channel_id=1, source_target_pairs={{0,4},{4,0},{8,12},{12,8},{1,5},{5,1},{9,13},{13,9},{2,6},{6,2},{1... | collective-permute-start | bytes 442376 | tf_op jit(solution)/shard_map/ppermute | solution.py:371
  22.4 7.1 %collective-permute-start.6 = (bf16[240,96]{1,0:T(8,128)(2,1)S(1)}, bf16[240,96]{1,0:T(8,128)(2,1)S(1)}, u32[]{:S(2)}, u32[]{:S(2)}) collective-permute-start(bf16[240,96]{1,0:T(8,128)(2,1)S(1)} %get-tuple-element.22), channel_id=1, source_target_pairs={{0,1},{1,0},{2,3},{3,2},{4,5},{5,4},{6,7},{7,6},{8,9},{9,8},{10,11... | collective-permute-start | bytes 138248 | tf_op jit(solution)/shard_map/ppermute | solution.py:371
  22.4 7.1 %collective-permute-start.7 = (bf16[240,96]{1,0:T(8,128)(2,1)S(1)}, bf16[240,96]{1,0:T(8,128)(2,1)S(1)}, u32[]{:S(2)}, u32[]{:S(2)}) collective-permute-start(bf16[240,96]{1,0:T(8,128)(2,1)S(1)} %get-tuple-element.23), channel_id=1, source_target_pairs={{0,3},{1,2},{2,1},{3,0},{4,7},{5,6},{6,5},{7,4},{8,11},{9,10},{10,... | collective-permute-start | bytes 138248 | tf_op jit(solution)/shard_map/ppermute | solution.py:371
  23.2 6.3 %collective-permute-start.8 = (bf16[48,96]{1,0:T(8,128)(2,1)S(1)}, bf16[48,96]{1,0:T(8,128)(2,1)S(1)}, u32[]{:S(2)}, u32[]{:S(2)}) collective-permute-start(bf16[48,96]{1,0:T(8,128)(2,1)S(1)} %get-tuple-element.24.own_ref), channel_id=1, source_target_pairs={{0,2},{1,3},{2,0},{3,1},{4,6},{5,7},{6,4},{7,5},{8,10},{9,11},{10,... | collective-permute-start | bytes 27656 | tf_op jit(solution)/shard_map/ppermute | solution.py:371
  29.5 8.2 %copy-start.8 = (f32[96]{0:T(128)S(1)}, f32[96]{0:T(128)}, u32[]{:S(2)}) copy-start(f32[96]{0:T(128)} %bias_ref.3) | copy-start | bytes 1156
  29.8 2.0 %collective-permute-start.9 = (bf16[3,4,48,128]{3,2,1,0:T(8,128)(2,1)S(1)}, bf16[3,4,48,128]{3,2,1,0:T(8,128)(2,1)S(1)}, u32[]{:S(2)}, u32[]{:S(2)}) collective-permute-start(bf16[3,4,48,128]{3,2,1,0:T(8,128)(2,1)S(1)} %shard_map.151.own_ref), channel_id=1, source_target_pairs={{0,4},{4,0},{8,12},{12,8},{1,5},{5,1},{9,13},{13,9},{2,6},{6,2},{1... | collective-permute-start | bytes 442376 | tf_op jit(solution)/shard_map/ppermute | solution.py:371
  29.9 6.3 %collective-permute-start.10 = (bf16[3,4,48,128]{3,2,1,0:T(8,128)(2,1)S(1)}, bf16[3,4,48,128]{3,2,1,0:T(8,128)(2,1)S(1)}, u32[]{:S(2)}, u32[]{:S(2)}) collective-permute-start(bf16[3,4,48,128]{3,2,1,0:T(8,128)(2,1)S(1)} %shard_map.151.own_ref), channel_id=1, source_target_pairs={{0,8},{4,12},{8,0},{12,4},{1,9},{5,13},{9,1},{13,5},{2,10},{6,14},... | collective-permute-start | bytes 442376 | tf_op jit(solution)/shard_map/ppermute | solution.py:371
  32.9 21.0 %copy-start.2 = (bf16[384,384]{1,0:T(8,128)(2,1)S(1)}, bf16[384,384]{1,0:T(8,128)(2,1)}, u32[]{:S(2)}) copy-start(bf16[384,384]{1,0:T(8,128)(2,1)} %refs_4_.1) | copy-start | bytes 884740
  32.9 21.0 %copy-start.3 = (bf16[384,384]{1,0:T(8,128)(2,1)S(1)}, bf16[384,384]{1,0:T(8,128)(2,1)}, u32[]{:S(2)}) copy-start(bf16[384,384]{1,0:T(8,128)(2,1)} %refs_5_.1) | copy-start | bytes 884740
  32.9 21.0 %copy-start.4 = (bf16[384,384]{1,0:T(8,128)(2,1)S(1)}, bf16[384,384]{1,0:T(8,128)(2,1)}, u32[]{:S(2)}) copy-start(bf16[384,384]{1,0:T(8,128)(2,1)} %refs_6_.1) | copy-start | bytes 884740
  32.9 21.0 %copy-start.5 = (bf16[384,384]{1,0:T(8,128)(2,1)S(1)}, bf16[384,384]{1,0:T(8,128)(2,1)}, u32[]{:S(2)}) copy-start(bf16[384,384]{1,0:T(8,128)(2,1)} %refs_7_.1) | copy-start | bytes 884740
  36.3 1.4 %collective-permute-start.11 = (bf16[3,4,48,128]{3,2,1,0:T(8,128)(2,1)S(1)}, bf16[3,4,48,128]{3,2,1,0:T(8,128)(2,1)S(1)}, u32[]{:S(2)}, u32[]{:S(2)}) collective-permute-start(bf16[3,4,48,128]{3,2,1,0:T(8,128)(2,1)S(1)} %shard_map.153), channel_id=1, source_target_pairs={{0,4},{4,0},{8,12},{12,8},{1,5},{5,1},{9,13},{13,9},{2,6},{6,2},{1... | collective-permute-start | bytes 442376 | tf_op jit(solution)/shard_map/ppermute | solution.py:371
  39.2 1.9 %collective-permute-start.12 = (bf16[96,96]{1,0:T(8,128)(2,1)S(1)}, bf16[96,96]{1,0:T(8,128)(2,1)S(1)}, u32[]{:S(2)}, u32[]{:S(2)}) collective-permute-start(bf16[96,96]{1,0:T(8,128)(2,1)S(1)} %get-tuple-element.26), channel_id=1, source_target_pairs={{0,4},{4,0},{8,12},{12,8},{1,5},{5,1},{9,13},{13,9},{2,6},{6,2},{1... | collective-permute-start | bytes 55304 | tf_op jit(solution)/shard_map/ppermute | solution.py:371
  39.4 3.8 %collective-permute-start.13 = (bf16[96,96]{1,0:T(8,128)(2,1)S(1)}, bf16[96,96]{1,0:T(8,128)(2,1)S(1)}, u32[]{:S(2)}, u32[]{:S(2)}) collective-permute-start(bf16[96,96]{1,0:T(8,128)(2,1)S(1)} %get-tuple-element.27), channel_id=1, source_target_pairs={{0,8},{4,12},{8,0},{12,4},{1,9},{5,13},{9,1},{13,5},{2,10},{6,14},... | collective-permute-start | bytes 55304 | tf_op jit(solution)/shard_map/ppermute | solution.py:371
  41.1 3.3 %collective-permute-start.14 = (bf16[96,96]{1,0:T(8,128)(2,1)S(1)}, bf16[96,96]{1,0:T(8,128)(2,1)S(1)}, u32[]{:S(2)}, u32[]{:S(2)}) collective-permute-start(bf16[96,96]{1,0:T(8,128)(2,1)S(1)} %get-tuple-element.28), channel_id=1, source_target_pairs={{0,12},{4,8},{8,4},{12,0},{1,13},{5,9},{9,5},{13,1},{2,14},{6,10},... | collective-permute-start | bytes 55304 | tf_op jit(solution)/shard_map/ppermute | solution.py:371
  44.5 7.0 %collective-permute-start.17 = (bf16[96,384]{1,0:T(8,128)(2,1)S(1)}, bf16[96,384]{1,0:T(8,128)(2,1)S(1)}, u32[]{:S(2)}, u32[]{:S(2)}) collective-permute-start(bf16[96,384]{1,0:T(8,128)(2,1)S(1)} %shard_map.155.own_ref), channel_id=1, source_target_pairs={{0,3},{1,2},{2,1},{3,0},{4,7},{5,6},{6,5},{7,4},{8,11},{9,10},{10,... | collective-permute-start | bytes 221192 | tf_op jit(solution)/shard_map/ppermute | solution.py:371
  46.0 7.8 %collective-permute-start.16 = (bf16[96,384]{1,0:T(8,128)(2,1)S(1)}, bf16[96,384]{1,0:T(8,128)(2,1)S(1)}, u32[]{:S(2)}, u32[]{:S(2)}) collective-permute-start(bf16[96,384]{1,0:T(8,128)(2,1)S(1)} %shard_map.155.own_ref), channel_id=1, source_target_pairs={{0,2},{1,3},{2,0},{3,1},{4,6},{5,7},{6,4},{7,5},{8,10},{9,11},{10,... | collective-permute-start | bytes 221192 | tf_op jit(solution)/shard_map/ppermute | solution.py:371
  46.5 7.4 %collective-permute-start.15 = (bf16[96,384]{1,0:T(8,128)(2,1)S(1)}, bf16[96,384]{1,0:T(8,128)(2,1)S(1)}, u32[]{:S(2)}, u32[]{:S(2)}) collective-permute-start(bf16[96,384]{1,0:T(8,128)(2,1)S(1)} %shard_map.155.own_ref), channel_id=1, source_target_pairs={{0,1},{1,0},{2,3},{3,2},{4,5},{5,4},{6,7},{7,6},{8,9},{9,8},{10,11... | collective-permute-start | bytes 221192 | tf_op jit(solution)/shard_map/ppermute | solution.py:371

commit v2 on v1

--- a/solution.py
+++ b/solution.py
@@ -59,15 +59,17 @@
     return mean, (sum(squares) + count * spread) / (count * len(means))
 
 
+def merge_blocks(blocks, step, count):
+    parts = [[b.astype(F32)[q * step : (q + 1) * step] for q in range(6)] for b in blocks]
+    return merge([p[0] + p[1] + p[2] for p in parts], [p[3] + p[4] + p[5] for p in parts], count)
+
+
 def silu(value):
     return value / (1.0 + jnp.exp(-value))
 
 
-def first_stats(r_ref, x_ref, near_ref, far_ref, own_ref, copy_ref):
-    _, rows, cols, channels = x_ref.shape
-    copy_ref[...] = x_ref[...]
-    x = x_ref[0].astype(F32).reshape(rows * cols, channels)
-    count = rows * cols * GROUP
+def plane_block(x, count):
+    channels = x.shape[1]
     mean = group_sums(jnp.broadcast_to(jnp.sum(x, axis=0, keepdims=True), (8, channels)))[0:1] / count
     square = group_sums(
         jnp.broadcast_to(jnp.sum(jnp.square(x - mean), axis=0, keepdims=True), (8, channels))
@@ -76,33 +78,49 @@
     block = jnp.zeros((16, channels), F32)
     for i, term in enumerate(split3(mean) + split3(square)):
         block = jnp.where(at == i, term, block)
-    block = block.astype(BF16)
+    return block.astype(BF16)
+
+
+def first_stats(r_ref, x_ref, near_ref, far_ref, own_ref, copy_ref):
+    _, rows, cols, channels = x_ref.shape
+    copy_ref[...] = x_ref[0]
+    own_ref[...] = plane_block(x_ref[0].astype(F32).reshape(rows * cols, channels), rows * cols * GROUP)
+    odd = r_ref[0] & 1
+    near_ref[...] = x_ref[0, (rows - 1) * (1 - odd)]
+    far_ref[...] = x_ref[0, (rows - 1) * odd]
+
+
+def pair_stats(r_ref, x_ref, mate_ref, loaded_ref, raw_ref, message_ref, own_ref):
+    _, rows, cols, channels = x_ref.shape
+    odd, half = r_ref[0] & 1, r_ref[0] >> 1
+    raw_ref[pl.ds(odd * rows, rows)] = x_ref[0]
+    raw_ref[pl.ds((1 - odd) * rows, rows)] = mate_ref[0]
+    wide = raw_ref[...].astype(F32).reshape(2 * rows * cols, channels)
+    block = plane_block(wide, 2 * rows * cols * GROUP)
     own_ref[...] = block
-    odd = r_ref[0] & 1
-    near_ref[0:cols] = x_ref[0, (rows - 1) * (1 - odd)]
-    near_ref[cols : cols + 16] = block
-    far_ref[0:cols] = x_ref[0, (rows - 1) * odd]
-    far_ref[cols : cols + 16] = block
-
-
-def load(w_ref, after_ref, out_ref, sem):
+    message_ref[0:cols] = raw_ref[(2 * rows - 1) * (1 - half)]
+    message_ref[cols : cols + 16] = block
+
+
+def pair_first_norm(raw_ref, message_ref, own_ref, table_ref, out_ref):
+    rows, cols, channels = raw_ref.shape
+    mean, variance = merge_blocks([own_ref[...], message_ref[cols : cols + 16]], 1, rows * cols * GROUP)
+    scale = lax.rsqrt(variance + EPSILON) * table_ref[0:1]
+    shift = table_ref[1:2]
+    for row in range(rows + 1):
+        value = raw_ref[row] if row < rows else message_ref[0:cols]
+        out_ref[0, row] = silu((value.astype(F32) - mean) * scale + shift).astype(BF16)
+
+
+def load(w_ref, out_ref, sem):
     copy = pltpu.make_async_copy(w_ref, out_ref, sem)
     copy.start()
     copy.wait()
 
 
-def first_norm(n, r_ref, x_ref, near_ref, far_ref, own_ref, table_ref, loaded_ref, *refs):
-    others, out_ref = refs[:-1], refs[-1]
+def first_norm(n, r_ref, x_ref, near_ref, far_ref, all_ref, table_ref, loaded_ref, out_ref):
     _, rows, cols, channels = x_ref.shape
-    blocks = [own_ref[...].astype(F32)]
-    if n == 4:
-        blocks += [near_ref[cols : cols + 16].astype(F32), far_ref[cols : cols + 16].astype(F32)]
-        blocks += [others[0][...].astype(F32)]
-    else:
-        blocks = [others[0][i].astype(F32) for i in range(n)]
-    means = [b[0:1] + b[1:2] + b[2:3] for b in blocks]
-    squares = [b[3:4] + b[4:5] + b[5:6] for b in blocks]
-    mean, variance = merge(means, squares, rows * cols * GROUP)
+    mean, variance = merge_blocks([all_ref[i] for i in range(n)], 1, rows * cols * GROUP)
     scale = lax.rsqrt(variance + EPSILON) * table_ref[0:1]
     shift = table_ref[1:2]
     r = r_ref[0]
@@ -158,32 +176,46 @@
     out_ref[...] = x_ref[...]
 
 
-def first_conv_near(m_ref, own_ref, mate_ref, w_ref, total_ref, pair):
-    odd = m_ref[0] & 1
-    pair[odd] = own_ref[0]
-    pair[1 - odd] = mate_ref[0]
+def lay_out(r_ref, m_ref, own_ref, mate_ref, pair):
+    odd, half = m_ref[0] & 1, r_ref[0] >> 1
+    rows = own_ref.shape[1] - 1
+    for at, ref in ((odd, own_ref), (1 - odd, mate_ref)):
+        pair[at, 1 : rows + 1] = ref[0, 0:rows]
+        pair[at, (rows + 1) * (1 - half)] = ref[0, rows]
+        pair[at, (rows + 1) * half] = jnp.zeros(ref.shape[2:], BF16)
+
+
+def first_conv_near(r_ref, m_ref, own_ref, mate_ref, w_ref, total_ref, pair):
+    lay_out(r_ref, m_ref, own_ref, mate_ref, pair)
     total_ref[...] = jnp.zeros(total_ref.shape, F32)
     on_half(m_ref, False, lambda h: add_taps(total_ref, pair, w_ref, slice(None), 2 * h, 2 * h + 2))
 
 
 def first_conv_rest(r_ref, m_ref, near_total_ref, own_ref, mate_ref, w_ref, bias_ref, *refs):
-    outs, (pair, total, rows8) = refs[:-3], refs[-3:]
-    odd = m_ref[0] & 1
-    pair[odd] = own_ref[0]
-    pair[1 - odd] = mate_ref[0]
+    out_ref, message_ref, block_ref, pair, total, rows8 = refs
+    lay_out(r_ref, m_ref, own_ref, mate_ref, pair)
     total[...] = near_total_ref[...]
     on_half(m_ref, True, lambda h: add_taps(total, pair, w_ref, slice(None), 2 * h, 2 * h + 2))
-    first_finish(r_ref, total, bias_ref, *outs, rows8)
-
-
-def first_conv(r_ref, a_ref, w_ref, bias_ref, *refs):
-    outs, (total, rows8) = refs[:-2], refs[-2:]
+    block = first_finish(total, bias_ref, out_ref, rows8)
+    frames, rows, cols, _ = out_ref.shape
+    block_ref[...] = block
+    for f in range(frames):
+        message_ref[f * cols : (f + 1) * cols] = out_ref[f, (rows - 1) * (1 - (r_ref[0] >> 1))]
+    message_ref[frames * cols :] = block
+
+
+def first_conv(r_ref, a_ref, w_ref, bias_ref, out_ref, near_ref, far_ref, block_ref, total, rows8):
     total[...] = jnp.zeros(total.shape, F32)
     add_taps(total, a_ref, w_ref, slice(None), 0, a_ref.shape[0])
-    first_finish(r_ref, total, bias_ref, *outs, rows8)
-
-
-def first_finish(r_ref, total_ref, bias_ref, out_ref, near_ref, far_ref, own_ref, rows8):
+    block_ref[...] = first_finish(total, bias_ref, out_ref, rows8)
+    frames, rows, cols, _ = out_ref.shape
+    odd = r_ref[0] & 1
+    for f in range(frames):
+        near_ref[f * cols : (f + 1) * cols] = out_ref[f, (rows - 1) * (1 - odd)]
+        far_ref[f * cols : (f + 1) * cols] = out_ref[f, (rows - 1) * odd]
+
+
+def first_finish(total_ref, bias_ref, out_ref, rows8):
     frames, rows, cols, outputs = out_ref.shape
     plane = rows * cols
     result = finish(total_ref, cols, bias_ref)
@@ -196,34 +228,14 @@
     for f in range(frames):
         rows8[f : f + 1] = jnp.sum(jnp.square(wide[f] - mean[f : f + 1]), axis=0, keepdims=True)
     square = group_sums(rows8[...])
-    block = jnp.concatenate(split3(mean) + split3(square), axis=0).astype(BF16)
-    size = block.shape[0]
-    own_ref[...] = block
-    odd = r_ref[0] & 1
-    for f in range(frames):
-        near_ref[f * cols : (f + 1) * cols] = out_ref[f, (rows - 1) * (1 - odd)]
-        far_ref[f * cols : (f + 1) * cols] = out_ref[f, (rows - 1) * odd]
-    near_ref[frames * cols : frames * cols + size] = block
-    far_ref[frames * cols : frames * cols + size] = block
-
-
-def second_norm(n, r_ref, m_ref, x_ref, near_ref, far_ref, own_ref, table_ref, *refs):
-    others, out_ref = refs[:-1], refs[-1]
+    return jnp.concatenate(split3(mean) + split3(square), axis=0).astype(BF16)
+
+
+def second_norm(n, r_ref, m_ref, x_ref, near_ref, far_ref, all_ref, table_ref, out_ref):
     frames, rows, cols, channels = x_ref.shape
     gain, shift = (own_part(table_ref[i : i + 1], m_ref[0], channels) for i in (2, 3))
     step = 8 * (-(-frames // 8))
-    size = 6 * step
-    base = frames * cols
-    blocks = [own_ref[...].astype(F32)]
-    if n == 4:
-        blocks += [near_ref[base : base + size].astype(F32), far_ref[base : base + size].astype(F32)]
-        blocks += [others[0][...].astype(F32)]
-    else:
-        blocks = [others[0][i].astype(F32) for i in range(n)]
-    parts = [[b[q * step : (q + 1) * step] for q in range(6)] for b in blocks]
-    means = [p[0] + p[1] + p[2] for p in parts]
-    squares = [p[3] + p[4] + p[5] for p in parts]
-    mean, variance = merge(means, squares, rows * cols * GROUP)
+    mean, variance = merge_blocks([all_ref[i] for i in range(n)], step, rows * cols * GROUP)
     scale = lax.rsqrt(variance + EPSILON) * gain
     r = r_ref[0]
     odd = r & 1
@@ -238,15 +250,45 @@
         far = jnp.where(beyond, 0.0, active(far_ref[f * cols : (f + 1) * cols]))
         above, below = jnp.where(odd == 1, near, far), jnp.where(odd == 1, far, near)
         planes.append([above] + [active(x_ref[f, row]) for row in range(rows)] + [below])
+    write_packed(planes, out_ref)
+
+
+def pair_second_norm(r_ref, m_ref, x_ref, message_ref, own_ref, table_ref, out_ref):
+    frames, rows, cols, channels = x_ref.shape
+    gain, shift = (own_part(table_ref[i : i + 1], m_ref[0], channels) for i in (2, 3))
+    base = frames * cols
+    size = own_ref.shape[0]
+    mean, variance = merge_blocks(
+        [own_ref[...], message_ref[base : base + size]], size // 6, rows * cols * GROUP
+    )
+    scale = lax.rsqrt(variance + EPSILON) * gain
+    odd, half = r_ref[0] & 1, r_ref[0] >> 1
+    planes = []
+    for f in range(frames):
+
+        def active(v):
+            return silu((v.astype(F32) - mean[f : f + 1]) * scale[f : f + 1] + shift)
+
+        rim = jnp.where(half != odd, active(message_ref[f * cols : (f + 1) * cols]), 0.0)
+        inner = active(x_ref[f, rows // 2 - odd])
+        above, below = jnp.where(odd == 1, inner, rim), jnp.where(odd == 1, rim, inner)
+        middle = [active(x_ref[f, rows // 2 * odd + row]) for row in range(rows // 2)]
+        planes.append([above] + middle + [below])
+    write_packed(planes, out_ref)
+
+
+def write_packed(planes, out_ref):
+    frames, channels = len(planes), planes[0][0].shape[1]
+    padded = len(planes[0])
     if packs(frames, channels):
         piece = channels // (frames - 1)
         for f in range(frames - 1):
-            for row in range(rows + 2):
+            for row in range(padded):
                 extra = planes[-1][row][:, f * piece : (f + 1) * piece]
                 out_ref[f, row] = jnp.concatenate([planes[f][row], extra], axis=1).astype(BF16)
     else:
         for f in range(frames):
-            for row in range(rows + 2):
+            for row in range(padded):
                 out_ref[f, row] = planes[f][row].astype(BF16)
 
 
@@ -328,13 +370,15 @@
         out_ref[...] = held[m_ref[0] ^ k]
 
 
-def add_hidden(m_ref, x_ref, *refs):
+def add_hidden(r_ref, m_ref, x_ref, *refs):
     parts, (out_ref, held) = refs[:-2], refs[-2:]
-    _, rows, cols, channels = x_ref.shape
+    held_rows, cols, channels = x_ref.shape
+    rows = out_ref.shape[0] // cols
+    start = (r_ref[0] & 1) * rows if held_rows > rows else 0
     for k, part in enumerate(parts):
         held[k] = part[...].astype(F32)
     update = jnp.concatenate([held[m_ref[0] ^ m] for m in range(len(parts))], axis=1)
-    out_ref[...] = (x_ref[0].reshape(rows * cols, channels).astype(F32) + update).astype(BF16)
+    out_ref[...] = (x_ref[pl.ds(start, rows)].reshape(rows * cols, channels).astype(F32) + update).astype(BF16)
 
 
 def attention(own_ref, *refs):
@@ -371,20 +415,12 @@
     return lax.ppermute(value, axis, [(i, partner(i)) for i in range(lax.axis_size(axis))])
 
 
-def far(i, n):
-    return ((i + 1) ^ 1) - 1 if 0 < i < n - 1 else n - 1 - i
-
-
-def around(near_message, far_message, own):
+def around(near, far, block):
     n = lax.axis_size("rows")
-    if n == 4:
-        others = [swapped(own, "rows", lambda i: i ^ 2)]
-    else:
-        others = [lax.all_gather(own, "rows")]
     return (
-        swapped(near_message, "rows", lambda i: i ^ 1),
-        swapped(far_message, "rows", functools.partial(far, n=n)),
-        others,
+        swapped(near, "rows", lambda i: i ^ 1),
+        swapped(far, "rows", lambda i: ((i + 1) ^ 1) - 1 if 0 < i < n - 1 else n - 1 - i),
+        lax.all_gather(block, "rows"),
     )
 
 
@@ -415,51 +451,67 @@
     def taps(kernel):
         return jnp.transpose(kernel, (1, 2, 3, 0, 4)).reshape(3, 3, 3 * outputs, channels)
 
-    message = struct((cols + 16, channels))
     row = lax.broadcasted_iota(jnp.int32, (8, channels), 0)
     table = jnp.zeros((8, channels), F32)
     for i, vector in enumerate([first_gain, first_shift, second_gain, second_shift, third_gain, third_shift]):
         table = jnp.where(row == i, vector[None, :], table)
-    near_message, far_message, own, features = call(
-        first_stats, (message, message, struct((16, channels)), struct(features.shape))
-    )(r, features)
-    near_message, far_message, others = around(near_message, far_message, own)
-    weights1 = taps(first_kernel)
-    weights1 = call(load, struct(weights1.shape), (pltpu.SemaphoreType.DMA,))(weights1, own)
-    active1 = call(functools.partial(first_norm, n), struct((1, rows + 2, cols, channels)))(
-        r, features, near_message, far_message, own, table, weights1, *others
-    )
-
+
+    weights1, weights2 = taps(first_kernel), taps(second_kernel)
+    weights1 = call(load, struct(weights1.shape), (pltpu.SemaphoreType.DMA,))(weights1)
     step = 8 * (-(-frames // 8))
     size = 6 * step
-    message = struct((frames * cols + size, outputs))
-    conv1_outs = (struct((frames, rows, cols, outputs)), message, message, struct((size, outputs)))
+    stats_scratch = pltpu.VMEM((step, outputs), F32)
     total = struct((frames * plane, 3 * outputs), F32)
     total_scratch = pltpu.VMEM(total.shape, F32)
-    stats_scratch = pltpu.VMEM((step, outputs), F32)
-    bias1, bias2 = first_bias, second_bias
-    split = frames == 4 and channels == 4 * outputs and 2 * outputs <= 256 < channels
+    active2_struct = struct(packed_shape(frames, rows + 2, cols, outputs))
+    split = n == 4 and frames == 4 and channels == 4 * outputs and 2 * outputs <= 256 < channels
     if split:
-        pair = pltpu.VMEM((2, rows + 2, cols, channels), BF16)
+        high = 2 * rows
+        mate_rows = swapped(features, "rows", lambda i: i ^ 1)
+        raw, message, block = call(
+            pair_stats,
+            (struct((high, cols, channels)), struct((cols + 16, channels)), struct((16, channels))),
+        )(r, features, mate_rows, weights1)
+        message = swapped(message, "rows", lambda i: i ^ 2)
+        active1 = call(pair_first_norm, struct((1, high + 1, cols, channels)))(raw, message, block, table)
+        pair = pltpu.VMEM((2, high + 2, cols, channels), BF16)
+        tall = struct((2 * frames * plane, 3 * outputs), F32)
         across = swapped(active1, "tm", lambda i: i ^ 2)
         mate = swapped(active1, "tm", lambda i: i ^ 1)
-        near_total = call(first_conv_near, total, (pair,))(m, active1, mate, weights1)
+        near_total = call(first_conv_near, tall, (pair,))(r, m, active1, mate, weights1)
         beside = swapped(call(hand_on, struct(across.shape))(across, near_total), "tm", lambda i: i ^ 1)
-        conv1, near_message, far_message, own = call(
-            first_conv_rest, conv1_outs, (pair, total_scratch, stats_scratch)
-        )(r, m, near_total, across, beside, weights1, bias1)
+        conv1, message, block = call(
+            first_conv_rest,
+            (
+                struct((frames, high, cols, outputs)),
+                struct((frames * cols + size, outputs)),
+                struct((size, outputs)),
+            ),
+            (pair, pltpu.VMEM(tall.shape, F32), stats_scratch),
+        )(r, m, near_total, across, beside, weights1, first_bias)
+        message = swapped(message, "rows", lambda i: i ^ 2)
+        active2 = call(pair_second_norm, active2_struct)(r, m, conv1, message, block, table)
     else:
+        halo = struct((cols, channels))
+        near, far, block, raw = call(
+            first_stats, (halo, halo, struct((16, channels)), struct((rows, cols, channels)))
+        )(r, features)
+        active1 = call(functools.partial(first_norm, n), struct((1, rows + 2, cols, channels)))(
+            r, features, *around(near, far, block), table, weights1
+        )
         clip = lax.all_gather(active1, "tm", axis=0, tiled=True)
-        conv1, near_message, far_message, own = call(first_conv, conv1_outs, (total_scratch, stats_scratch))(
-            r, clip, weights1, bias1
+        halo = struct((frames * cols, outputs))
+        conv1, near, far, block = call(
+            first_conv,
+            (struct((frames, rows, cols, outputs)), halo, halo, struct((size, outputs))),
+            (total_scratch, stats_scratch),
+        )(r, clip, weights1, first_bias)
+        active2 = call(functools.partial(second_norm, n), active2_struct)(
+            r, m, conv1, *around(near, far, block), table
         )
-    near_message, far_message, others = around(near_message, far_message, own)
-    active2 = call(functools.partial(second_norm, n), struct(packed_shape(frames, rows + 2, cols, outputs)))(
-        r, m, conv1, near_message, far_message, own, table, *others
-    )
+
     piece = struct((plane, outputs))
     held = pltpu.VMEM((frames, plane, outputs), BF16)
-    weights2 = taps(second_kernel)
     if split:
         both = pltpu.VMEM((2, *active2.shape), BF16)
         half = pltpu.VMEM((frames, rows + 2, cols, 256), BF16)
@@ -468,15 +520,15 @@
         near_total = call(second_conv_near, total, (both, half))(m, active2, mate, weights2)
         beside = swapped(call(hand_on, struct(across.shape))(across, near_total), "tm", lambda i: i ^ 1)
         pieces = call(second_conv_rest, [piece] * frames, (both, half, total_scratch, held))(
-            m, near_total, across, beside, weights2, bias2
+            m, near_total, across, beside, weights2, second_bias
         )
     else:
         parts = lax.all_gather(active2, "tm")
         whole = pltpu.VMEM((frames, rows + 2, cols, channels), BF16)
-        pieces = call(second_conv, [piece] * frames, (whole, total_scratch, held))(m, parts, weights2, bias2)
+        pieces = call(second_conv, [piece] * frames, (whole, total_scratch, held))(m, parts, weights2, second_bias)
     pieces = [pieces[0]] + [swapped(pieces[k], "tm", lambda i, k=k: i ^ k) for k in range(1, frames)]
     hidden = call(add_hidden, struct((plane, channels)), (pltpu.VMEM((frames, plane, outputs), F32),))(
-        m, features, *pieces
+        r, m, raw, *pieces
     )
     if n == 4:
         others = [swapped(hidden, "rows", lambda i, k=k: i ^ k) for k in (1, 2, 3)]

time: 56.3 us -> 56.3 us (level)
  starting transfers between devices: 19.4 us -> 21.4 us
  waiting for transfers between devices: 24.5 us -> 22.8 us
  Pallas kernels: 8.65 us -> 9.97 us
  local copies, waits for them, and re-layouts: 2.47 us -> 1.63 us
  other arithmetic: 0.86 us -> 0.1 us
    ppermute x18 -> x15, starting transfers between devices: 19.4 us -> 21.4 us  [swapped(): lax.ppermute(value, axis, [(i, partner(i)) for i in range(lax.axis_size(a...]
    ppermute x18 -> x15, waiting for transfers between devices: 24.5 us -> 22.8 us  [swapped(): lax.ppermute(value, axis, [(i, partner(i)) for i in range(lax.axis_size(a...]
    pallas_call x12, Pallas kernels: 8.65 us -> 9.97 us  [run(): pl.pallas_call(body, out_shape=outs, in_specs=[SMEM if a.dtype == jnp.int...]
    unnamed x18 -> x30, local copies, waits for them, and re-layouts: 2.47 us -> 1.63 us
    select_n x1, other arithmetic: 0.85 us -> 0.08 us  [per_device(): table = jnp.where(row == i, vector[None, :], table)]
  transfers between devices with their start and end apart: 18 -> 15, of which waited for: 10 -> 12; matrix products, arithmetic and copies ran while one was open for 2% -> 0% of each run, Pallas kernels for 4% -> 6%
where the time goes in v2:
time: 56.3 us; the launch traced here: 56.1 us
  waiting for transfers between devices  22.8 us (40%)
  starting transfers between devices  21.4 us (38%)
  Pallas kernels  9.97 us (18%)
  local copies, waits for them, and re-layouts  1.63 us (3%)
    ppermute x15, waiting for transfers between devices, swapped(): lax.ppermute(value, axis, [(i, partner(i)) for i in range(lax.axis_size(a...  22.8 us
    ppermute x15, starting transfers between devices, swapped(): lax.ppermute(value, axis, [(i, partner(i)) for i in range(lax.axis_size(a...  21.4 us
    pallas_call x12, Pallas kernels, run(): pl.pallas_call(body, out_shape=outs, in_specs=[SMEM if a.dtype == jnp.int...  9.97 us
    unnamed x30, local copies, waits for them, and re-layouts  1.63 us
  transfers between devices with their start and end apart: 15, of which 12 were waited for; matrix products, arithmetic and copies ran while one was open for 0% of the time, Pallas kernels for 6%

profile of v2, /device:TPU:0, one launch (start us, length us, event | category | flops | bytes accessed | tf_op | source)
XLA Modules:
  0.0 56.1 jit_solution(14534726377570494925)
XLA Ops:
  0.0 3.0 %collective-permute-start = (bf16[1,2,48,384]{3,2,1,0:T(8,128)(2,1)}, bf16[1,2,48,384]{3,2,1,0:T(8,128)(2,1)S(1)}, u32[]{:S(2)}, u32[]{:S(2)}) collective-permute-start(bf16[1,2,48,384]{3,2,1,0:T(8,128)(2,1)} %x_ref.1), channel_id=1, source_target_pairs={{0,1},{1,0},{2,3},{3,2},{4,5},{5,4},{6,7},{7,6},{8,9},{9,8},{10,11... | collective-permute-start | bytes 221192 | tf_op jit(solution)/shard_map/ppermute | solution.py:415
  3.0 0.0 copy-start.1
  3.1 1.5 %copy-done.1 = bf16[96,3,3,3,384]{4,0,3,2,1:T(8,128)(2,1)S(1)} copy-done((bf16[96,3,3,3,384]{4,0,3,2,1:T(8,128)(2,1)S(1)}, bf16[96,3,3,3,384]{4,0,3,2,1:T(8,128)(2,1)}, u32[]{:S(2)}) %copy-start.1) | copy-done | bytes 1990680
  4.6 0.3 shard_map.145.loaded_ref.w_ref
  4.9 0.0 copy-start.9
  5.0 0.0 copy-start.10
  5.0 0.0 copy-start.11
  5.0 0.0 copy-start.12
  5.0 0.0 copy-start.13
  5.0 0.0 copy-start.14
  5.0 0.5 collective-permute-done.mate_ref
  5.6 0.4 shard_map.146
  6.0 3.1 %collective-permute-start.1 = (bf16[64,384]{1,0:T(8,128)(2,1)S(1)}, bf16[64,384]{1,0:T(8,128)(2,1)S(1)}, u32[]{:S(2)}, u32[]{:S(2)}) collective-permute-start(bf16[64,384]{1,0:T(8,128)(2,1)S(1)} %get-tuple-element.16), channel_id=1, source_target_pairs={{0,2},{1,3},{2,0},{3,1},{4,6},{5,7},{6,4},{7,5},{8,10},{9,11},{10,... | collective-permute-start | bytes 147464 | tf_op jit(solution)/shard_map/ppermute | solution.py:415
  9.1 0.1 select_select_fusion.table_ref.refs_3_
  9.2 2.0 %collective-permute-done.1.message_ref = bf16[64,384]{1,0:T(8,128)(2,1)S(1)} collective-permute-done((bf16[64,384]{1,0:T(8,128)(2,1)S(1)}, bf16[64,384]{1,0:T(8,128)(2,1)S(1)}, u32[]{:S(2)}, u32[]{:S(2)}) %collective-permute-start.1) | collective-permute-done | bytes 49184 | tf_op jit(solution)/shard_map/ppermute | solution.py:415
  11.2 0.2 shard_map.147.own_ref
  11.3 0.1 collective-permute-start.2
  11.4 1.9 %collective-permute-start.3 = (bf16[1,5,48,384]{3,2,1,0:T(8,128)(2,1)S(1)}, bf16[1,5,48,384]{3,2,1,0:T(8,128)(2,1)S(1)}, u32[]{:S(2)}, u32[]{:S(2)}) collective-permute-start(bf16[1,5,48,384]{3,2,1,0:T(8,128)(2,1)S(1)} %shard_map.147.own_ref), channel_id=1, source_target_pairs={{0,8},{4,12},{8,0},{12,4},{1,9},{5,13},{9,1},{13,5},{2,10},{6,14},... | collective-permute-start | bytes 552968 | tf_op jit(solution)/shard_map/ppermute | solution.py:415
  13.3 1.7 %shard_map.148.after_ref.near_total_ref = f32[768,288]{1,0:T(8,128)S(1)} custom-call(s32[1]{0:T(128)} %bitcast.r_ref, s32[1]{0:T(128)} %bitcast.1.m_ref, bf16[1,5,48,384]{3,2,1,0:T(8,128)(2,1)S(1)} %shard_map.147.own_ref, bf16[1,5,48,384]{3,2,1,0:T(8,128)(2,1)S(1)} %collective-permute-done.2.mate_ref, bf16[3,3,288,384]{3,2,1,0:T(8,128)(2,1)S(1)} %shard_map.145.loaded_ref.w_ref), custom_call_target="tpu_custom_call" | custom-call | tf_op jit(solution)/shard_map/pallas_call | solution.py:22
  15.1 3.5 %collective-permute-done.3.x_ref.own_ref = bf16[1,5,48,384]{3,2,1,0:T(8,128)(2,1)S(1)} collective-permute-done((bf16[1,5,48,384]{3,2,1,0:T(8,128)(2,1)S(1)}, bf16[1,5,48,384]{3,2,1,0:T(8,128)(2,1)S(1)}, u32[]{:S(2)}, u32[]{:S(2)}) %collective-permute-start.3) | collective-permute-done | bytes 184352 | tf_op jit(solution)/shard_map/ppermute | solution.py:415
  18.6 0.0 copy-start
  18.6 0.1 collective-permute-start.4
  18.6 1.4 %collective-permute-done.4.mate_ref = bf16[1,5,48,384]{3,2,1,0:T(8,128)(2,1)S(1)} collective-permute-done((bf16[1,5,48,384]{3,2,1,0:T(8,128)(2,1)S(1)}, bf16[1,5,48,384]{3,2,1,0:T(8,128)(2,1)S(1)}, u32[]{:S(2)}, u32[]{:S(2)}) %collective-permute-start.4) | collective-permute-done | bytes 184352 | tf_op jit(solution)/shard_map/ppermute | solution.py:415
  20.1 2.2 %shard_map.150 = (bf16[4,4,48,96]{3,2,1,0:T(8,128)(2,1)S(1)}, bf16[240,96]{1,0:T(8,128)(2,1)S(1)}, bf16[48,96]{1,0:T(8,128)(2,1)S(1)}) custom-call(s32[1]{0:T(128)} %bitcast.r_ref, s32[1]{0:T(128)} %bitcast.1.m_ref, f32[768,288]{1,0:T(8,128)S(1)} %shard_map.148.after_ref.near_total_ref, bf16[1,5,48,384]{3,2,1,0:T(8,128)(2,1)S(1)} %collective-permute-done.3.x_ref.own_ref, ...), custom_call_target="tpu_custom_call" | custom-call | tf_op jit(solution)/shard_map/pallas_call | solution.py:22
  22.2 3.0 %collective-permute-start.5 = (bf16[240,96]{1,0:T(8,128)(2,1)S(1)}, bf16[240,96]{1,0:T(8,128)(2,1)S(1)}, u32[]{:S(2)}, u32[]{:S(2)}) collective-permute-start(bf16[240,96]{1,0:T(8,128)(2,1)S(1)} %get-tuple-element.19), channel_id=1, source_target_pairs={{0,2},{1,3},{2,0},{3,1},{4,6},{5,7},{6,4},{7,5},{8,10},{9,11},{10,... | collective-permute-start | bytes 138248 | tf_op jit(solution)/shard_map/ppermute | solution.py:415
  25.2 2.3 %collective-permute-done.5.message_ref = bf16[240,96]{1,0:T(8,128)(2,1)S(1)} collective-permute-done((bf16[240,96]{1,0:T(8,128)(2,1)S(1)}, bf16[240,96]{1,0:T(8,128)(2,1)S(1)}, u32[]{:S(2)}, u32[]{:S(2)}) %collective-permute-start.5) | collective-permute-done | bytes 46112 | tf_op jit(solution)/shard_map/ppermute | solution.py:415
  27.5 0.3 shard_map.151.own_ref
  27.8 0.1 collective-permute-start.6
  27.9 3.7 %collective-permute-start.7 = (bf16[3,4,48,128]{3,2,1,0:T(8,128)(2,1)S(1)}, bf16[3,4,48,128]{3,2,1,0:T(8,128)(2,1)S(1)}, u32[]{:S(2)}, u32[]{:S(2)}) collective-permute-start(bf16[3,4,48,128]{3,2,1,0:T(8,128)(2,1)S(1)} %shard_map.151.own_ref), channel_id=1, source_target_pairs={{0,8},{4,12},{8,0},{12,4},{1,9},{5,13},{9,1},{13,5},{2,10},{6,14},... | collective-permute-start | bytes 442376 | tf_op jit(solution)/shard_map/ppermute | solution.py:415
  31.6 1.0 %shard_map.152.after_ref.near_total_ref = f32[384,288]{1,0:T(8,128)S(1)} custom-call(s32[1]{0:T(128)} %bitcast.1.m_ref, bf16[3,4,48,128]{3,2,1,0:T(8,128)(2,1)S(1)} %shard_map.151.own_ref, bf16[3,4,48,128]{3,2,1,0:T(8,128)(2,1)S(1)} %collective-permute-done.6.mate_ref, bf16[3,3,288,384]{3,2,1,0:T(8,128)(2,1)S(1)} %bitcast.9), custom_call_target="tpu_custom_call" | custom-call | tf_op jit(solution)/shard_map/pallas_call | solution.py:22
  32.7 0.0 copy-start.3
  32.7 0.0 copy-start.4
  32.7 3.3 %collective-permute-done.7.x_ref.own_ref = bf16[3,4,48,128]{3,2,1,0:T(8,128)(2,1)S(1)} collective-permute-done((bf16[3,4,48,128]{3,2,1,0:T(8,128)(2,1)S(1)}, bf16[3,4,48,128]{3,2,1,0:T(8,128)(2,1)S(1)}, u32[]{:S(2)}, u32[]{:S(2)}) %collective-permute-start.7) | collective-permute-done | bytes 147488 | tf_op jit(solution)/shard_map/ppermute | solution.py:415
  36.1 0.1 collective-permute-start.8
  36.2 1.4 %collective-permute-done.8.mate_ref = bf16[3,4,48,128]{3,2,1,0:T(8,128)(2,1)S(1)} collective-permute-done((bf16[3,4,48,128]{3,2,1,0:T(8,128)(2,1)S(1)}, bf16[3,4,48,128]{3,2,1,0:T(8,128)(2,1)S(1)}, u32[]{:S(2)}, u32[]{:S(2)}) %collective-permute-start.8) | collective-permute-done | bytes 147488 | tf_op jit(solution)/shard_map/ppermute | solution.py:415
  37.5 1.5 %shard_map.154 = (bf16[96,96]{1,0:T(8,128)(2,1)S(1)}, bf16[96,96]{1,0:T(8,128)(2,1)S(1)}, bf16[96,96]{1,0:T(8,128)(2,1)S(1)}, bf16[96,96]{1,0:T(8,128)(2,1)S(1)}) custom-call(s32[1]{0:T(128)} %bitcast.1.m_ref, f32[384,288]{1,0:T(8,128)S(1)} %shard_map.152.after_ref.near_total_ref, bf16[3,4,48,128]{3,2,1,0:T(8,128)(2,1)S(1)} %collective-permute-done.7.x_ref.own_ref, ...), custom_call_target="tpu_custom_call" | custom-call | tf_op jit(solution)/shard_map/pallas_call | solution.py:22
  39.0 0.2 collective-permute-start.9
  39.2 1.7 %collective-permute-start.10 = (bf16[96,96]{1,0:T(8,128)(2,1)S(1)}, bf16[96,96]{1,0:T(8,128)(2,1)S(1)}, u32[]{:S(2)}, u32[]{:S(2)}) collective-permute-start(bf16[96,96]{1,0:T(8,128)(2,1)S(1)} %get-tuple-element.23), channel_id=1, source_target_pairs={{0,8},{4,12},{8,0},{12,4},{1,9},{5,13},{9,1},{13,5},{2,10},{6,14},... | collective-permute-start | bytes 55304 | tf_op jit(solution)/shard_map/ppermute | solution.py:415
  40.9 0.0 collective-permute-start.11
  41.0 2.1 %collective-permute-done.10.refs_2_ = bf16[96,96]{1,0:T(8,128)(2,1)S(1)} collective-permute-done((bf16[96,96]{1,0:T(8,128)(2,1)S(1)}, bf16[96,96]{1,0:T(8,128)(2,1)S(1)}, u32[]{:S(2)}, u32[]{:S(2)}) %collective-permute-start.10) | collective-permute-done | bytes 18464 | tf_op jit(solution)/shard_map/ppermute | solution.py:415
  43.1 1.1 %collective-permute-done.11.refs_3_ = bf16[96,96]{1,0:T(8,128)(2,1)S(1)} collective-permute-done((bf16[96,96]{1,0:T(8,128)(2,1)S(1)}, bf16[96,96]{1,0:T(8,128)(2,1)S(1)}, u32[]{:S(2)}, u32[]{:S(2)}) %collective-permute-start.11) | collective-permute-done | bytes 18464 | tf_op jit(solution)/shard_map/ppermute | solution.py:415
  44.2 0.1 shard_map.155.own_ref
  44.3 3.4 %collective-permute-start.14 = (bf16[96,384]{1,0:T(8,128)(2,1)S(1)}, bf16[96,384]{1,0:T(8,128)(2,1)S(1)}, u32[]{:S(2)}, u32[]{:S(2)}) collective-permute-start(bf16[96,384]{1,0:T(8,128)(2,1)S(1)} %shard_map.155.own_ref), channel_id=1, source_target_pairs={{0,3},{1,2},{2,1},{3,0},{4,7},{5,6},{6,5},{7,4},{8,11},{9,10},{10,... | collective-permute-start | bytes 221192 | tf_op jit(solution)/shard_map/ppermute | solution.py:415
  47.8 1.0 %collective-permute-start.12 = (bf16[96,384]{1,0:T(8,128)(2,1)S(1)}, bf16[96,384]{1,0:T(8,128)(2,1)S(1)}, u32[]{:S(2)}, u32[]{:S(2)}) collective-permute-start(bf16[96,384]{1,0:T(8,128)(2,1)S(1)} %shard_map.155.own_ref), channel_id=1, source_target_pairs={{0,1},{1,0},{2,3},{3,2},{4,5},{5,4},{6,7},{7,6},{8,9},{9,8},{10,11... | collective-permute-start | bytes 221192 | tf_op jit(solution)/shard_map/ppermute | solution.py:415
  48.8 2.6 %collective-permute-done.14.refs_2_ = bf16[96,384]{1,0:T(8,128)(2,1)S(1)} collective-permute-done((bf16[96,384]{1,0:T(8,128)(2,1)S(1)}, bf16[96,384]{1,0:T(8,128)(2,1)S(1)}, u32[]{:S(2)}, u32[]{:S(2)}) %collective-permute-start.14) | collective-permute-done | bytes 73760 | tf_op jit(solution)/shard_map/ppermute | solution.py:415
  51.4 2.4 %collective-permute-done.13.refs_1_ = bf16[96,384]{1,0:T(8,128)(2,1)S(1)} collective-permute-done((bf16[96,384]{1,0:T(8,128)(2,1)S(1)}, bf16[96,384]{1,0:T(8,128)(2,1)S(1)}, u32[]{:S(2)}, u32[]{:S(2)}) %collective-permute-start.13) | collective-permute-done | bytes 73760 | tf_op jit(solution)/shard_map/ppermute | solution.py:415
  53.7 0.2 collective-permute-done.12.refs_0_
  53.9 2.2 %shard_map.156 = bf16[96,384]{1,0:T(8,128)(2,1)} custom-call(bf16[96,384]{1,0:T(8,128)(2,1)S(1)} %shard_map.155.own_ref, bf16[96,384]{1,0:T(8,128)(2,1)S(1)} %collective-permute-done.12.refs_0_, bf16[96,384]{1,0:T(8,128)(2,1)S(1)} %collective-permute-done.13.refs_1_, bf16[96,384]{1,0:T(8,128)(2,1)S(1)} %collective-permute-done.14.refs_2_, ...), custom_call_target="tpu_custom_call" | custom-call | tf_op jit(solution)/shard_map/pallas_call | solution.py:22
  (28 shorter events, 0.1 us)
Async XLA Ops:
  0.0 5.6 %collective-permute-start = (bf16[1,2,48,384]{3,2,1,0:T(8,128)(2,1)}, bf16[1,2,48,384]{3,2,1,0:T(8,128)(2,1)S(1)}, u32[]{:S(2)}, u32[]{:S(2)}) collective-permute-start(bf16[1,2,48,384]{3,2,1,0:T(8,128)(2,1)} %x_ref.1), channel_id=1, source_target_pairs={{0,1},{1,0},{2,3},{3,2},{4,5},{5,4},{6,7},{7,6},{8,9},{9,8},{10,11... | collective-permute-start | bytes 221192 | tf_op jit(solution)/shard_map/ppermute | solution.py:415
  3.0 1.6 %copy-start.1 = (bf16[96,3,3,3,384]{4,0,3,2,1:T(8,128)(2,1)S(1)}, bf16[96,3,3,3,384]{4,0,3,2,1:T(8,128)(2,1)}, u32[]{:S(2)}) copy-start(bf16[96,3,3,3,384]{4,0,3,2,1:T(8,128)(2,1)} %param.18) | copy-start | bytes 5971972
  4.6 1.0 %copy-start.6 = (bf16[1,2,48,384]{3,2,1,0:T(8,128)(2,1)S(1)}, bf16[1,2,48,384]{3,2,1,0:T(8,128)(2,1)}, u32[]{:S(2)}) copy-start(bf16[1,2,48,384]{3,2,1,0:T(8,128)(2,1)} %x_ref.1) | copy-start | bytes 221188
  4.9 4.2 %copy-start.9 = (f32[384]{0:T(512)S(1)}, f32[384]{0:T(512)}, u32[]{:S(2)}) copy-start(f32[384]{0:T(512)} %param.16) | copy-start | bytes 4612
  5.0 4.2 %copy-start.10 = (f32[384]{0:T(512)S(1)}, f32[384]{0:T(512)}, u32[]{:S(2)}) copy-start(f32[384]{0:T(512)} %param.17) | copy-start | bytes 4612
  5.0 4.2 %copy-start.11 = (f32[384]{0:T(512)S(1)}, f32[384]{0:T(512)}, u32[]{:S(2)}) copy-start(f32[384]{0:T(512)} %param.20) | copy-start | bytes 4612
  5.0 4.2 %copy-start.12 = (f32[384]{0:T(512)S(1)}, f32[384]{0:T(512)}, u32[]{:S(2)}) copy-start(f32[384]{0:T(512)} %param.21) | copy-start | bytes 4612
  5.0 4.1 %copy-start.13 = (f32[384]{0:T(512)S(1)}, f32[384]{0:T(512)}, u32[]{:S(2)}) copy-start(f32[384]{0:T(512)} %param.24) | copy-start | bytes 4612
  5.0 4.1 %copy-start.14 = (f32[384]{0:T(512)S(1)}, f32[384]{0:T(512)}, u32[]{:S(2)}) copy-start(f32[384]{0:T(512)} %param.25) | copy-start | bytes 4612
  6.0 5.2 %collective-permute-start.1 = (bf16[64,384]{1,0:T(8,128)(2,1)S(1)}, bf16[64,384]{1,0:T(8,128)(2,1)S(1)}, u32[]{:S(2)}, u32[]{:S(2)}) collective-permute-start(bf16[64,384]{1,0:T(8,128)(2,1)S(1)} %get-tuple-element.16), channel_id=1, source_target_pairs={{0,2},{1,3},{2,0},{3,1},{4,6},{5,7},{6,4},{7,5},{8,10},{9,11},{10,... | collective-permute-start | bytes 147464 | tf_op jit(solution)/shard_map/ppermute | solution.py:415
  11.3 2.0 %collective-permute-start.2 = (bf16[1,5,48,384]{3,2,1,0:T(8,128)(2,1)S(1)}, bf16[1,5,48,384]{3,2,1,0:T(8,128)(2,1)S(1)}, u32[]{:S(2)}, u32[]{:S(2)}) collective-permute-start(bf16[1,5,48,384]{3,2,1,0:T(8,128)(2,1)S(1)} %shard_map.147.own_ref), channel_id=1, source_target_pairs={{0,4},{4,0},{8,12},{12,8},{1,5},{5,1},{9,13},{13,9},{2,6},{6,2},{1... | collective-permute-start | bytes 552968 | tf_op jit(solution)/shard_map/ppermute | solution.py:415
  11.4 7.1 %collective-permute-start.3 = (bf16[1,5,48,384]{3,2,1,0:T(8,128)(2,1)S(1)}, bf16[1,5,48,384]{3,2,1,0:T(8,128)(2,1)S(1)}, u32[]{:S(2)}, u32[]{:S(2)}) collective-permute-start(bf16[1,5,48,384]{3,2,1,0:T(8,128)(2,1)S(1)} %shard_map.147.own_ref), channel_id=1, source_target_pairs={{0,8},{4,12},{8,0},{12,4},{1,9},{5,13},{9,1},{13,5},{2,10},{6,14},... | collective-permute-start | bytes 552968 | tf_op jit(solution)/shard_map/ppermute | solution.py:415
  13.3 6.8 %copy-start.7 = (f32[96]{0:T(128)S(1)}, f32[96]{0:T(128)}, u32[]{:S(2)}) copy-start(f32[96]{0:T(128)} %bias_ref.2) | copy-start | bytes 1156
  18.6 13.1 %copy-start = (bf16[96,3,3,3,384]{4,0,3,2,1:T(8,128)(2,1)S(1)}, bf16[96,3,3,3,384]{4,0,3,2,1:T(8,128)(2,1)}, u32[]{:S(2)}) copy-start(bf16[96,3,3,3,384]{4,0,3,2,1:T(8,128)(2,1)} %param.22) | copy-start | bytes 5971972
  18.6 1.5 %collective-permute-start.4 = (bf16[1,5,48,384]{3,2,1,0:T(8,128)(2,1)S(1)}, bf16[1,5,48,384]{3,2,1,0:T(8,128)(2,1)S(1)}, u32[]{:S(2)}, u32[]{:S(2)}) collective-permute-start(bf16[1,5,48,384]{3,2,1,0:T(8,128)(2,1)S(1)} %shard_map.149), channel_id=1, source_target_pairs={{0,4},{4,0},{8,12},{12,8},{1,5},{5,1},{9,13},{13,9},{2,6},{6,2},{1... | collective-permute-start | bytes 552968 | tf_op jit(solution)/shard_map/ppermute | solution.py:415
  22.2 5.3 %collective-permute-start.5 = (bf16[240,96]{1,0:T(8,128)(2,1)S(1)}, bf16[240,96]{1,0:T(8,128)(2,1)S(1)}, u32[]{:S(2)}, u32[]{:S(2)}) collective-permute-start(bf16[240,96]{1,0:T(8,128)(2,1)S(1)} %get-tuple-element.19), channel_id=1, source_target_pairs={{0,2},{1,3},{2,0},{3,1},{4,6},{5,7},{6,4},{7,5},{8,10},{9,11},{10,... | collective-permute-start | bytes 138248 | tf_op jit(solution)/shard_map/ppermute | solution.py:415
  27.5 10.0 %copy-start.8 = (f32[96]{0:T(128)S(1)}, f32[96]{0:T(128)}, u32[]{:S(2)}) copy-start(f32[96]{0:T(128)} %bias_ref.3) | copy-start | bytes 1156
  27.8 3.8 %collective-permute-start.6 = (bf16[3,4,48,128]{3,2,1,0:T(8,128)(2,1)S(1)}, bf16[3,4,48,128]{3,2,1,0:T(8,128)(2,1)S(1)}, u32[]{:S(2)}, u32[]{:S(2)}) collective-permute-start(bf16[3,4,48,128]{3,2,1,0:T(8,128)(2,1)S(1)} %shard_map.151.own_ref), channel_id=1, source_target_pairs={{0,4},{4,0},{8,12},{12,8},{1,5},{5,1},{9,13},{13,9},{2,6},{6,2},{1... | collective-permute-start | bytes 442376 | tf_op jit(solution)/shard_map/ppermute | solution.py:415
  27.9 8.2 %collective-permute-start.7 = (bf16[3,4,48,128]{3,2,1,0:T(8,128)(2,1)S(1)}, bf16[3,4,48,128]{3,2,1,0:T(8,128)(2,1)S(1)}, u32[]{:S(2)}, u32[]{:S(2)}) collective-permute-start(bf16[3,4,48,128]{3,2,1,0:T(8,128)(2,1)S(1)} %shard_map.151.own_ref), channel_id=1, source_target_pairs={{0,8},{4,12},{8,0},{12,4},{1,9},{5,13},{9,1},{13,5},{2,10},{6,14},... | collective-permute-start | bytes 442376 | tf_op jit(solution)/shard_map/ppermute | solution.py:415
  32.7 21.2 %copy-start.2 = (bf16[384,384]{1,0:T(8,128)(2,1)S(1)}, bf16[384,384]{1,0:T(8,128)(2,1)}, u32[]{:S(2)}) copy-start(bf16[384,384]{1,0:T(8,128)(2,1)} %refs_4_.1) | copy-start | bytes 884740
  32.7 21.2 %copy-start.3 = (bf16[384,384]{1,0:T(8,128)(2,1)S(1)}, bf16[384,384]{1,0:T(8,128)(2,1)}, u32[]{:S(2)}) copy-start(bf16[384,384]{1,0:T(8,128)(2,1)} %refs_5_.1) | copy-start | bytes 884740
  32.7 21.2 %copy-start.4 = (bf16[384,384]{1,0:T(8,128)(2,1)S(1)}, bf16[384,384]{1,0:T(8,128)(2,1)}, u32[]{:S(2)}) copy-start(bf16[384,384]{1,0:T(8,128)(2,1)} %refs_6_.1) | copy-start | bytes 884740
  32.7 21.2 %copy-start.5 = (bf16[384,384]{1,0:T(8,128)(2,1)S(1)}, bf16[384,384]{1,0:T(8,128)(2,1)}, u32[]{:S(2)}) copy-start(bf16[384,384]{1,0:T(8,128)(2,1)} %refs_7_.1) | copy-start | bytes 884740
  36.1 1.4 %collective-permute-start.8 = (bf16[3,4,48,128]{3,2,1,0:T(8,128)(2,1)S(1)}, bf16[3,4,48,128]{3,2,1,0:T(8,128)(2,1)S(1)}, u32[]{:S(2)}, u32[]{:S(2)}) collective-permute-start(bf16[3,4,48,128]{3,2,1,0:T(8,128)(2,1)S(1)} %shard_map.153), channel_id=1, source_target_pairs={{0,4},{4,0},{8,12},{12,8},{1,5},{5,1},{9,13},{13,9},{2,6},{6,2},{1... | collective-permute-start | bytes 442376 | tf_op jit(solution)/shard_map/ppermute | solution.py:415
  39.0 1.9 %collective-permute-start.9 = (bf16[96,96]{1,0:T(8,128)(2,1)S(1)}, bf16[96,96]{1,0:T(8,128)(2,1)S(1)}, u32[]{:S(2)}, u32[]{:S(2)}) collective-permute-start(bf16[96,96]{1,0:T(8,128)(2,1)S(1)} %get-tuple-element.22), channel_id=1, source_target_pairs={{0,4},{4,0},{8,12},{12,8},{1,5},{5,1},{9,13},{13,9},{2,6},{6,2},{1... | collective-permute-start | bytes 55304 | tf_op jit(solution)/shard_map/ppermute | solution.py:415
  39.2 3.8 %collective-permute-start.10 = (bf16[96,96]{1,0:T(8,128)(2,1)S(1)}, bf16[96,96]{1,0:T(8,128)(2,1)S(1)}, u32[]{:S(2)}, u32[]{:S(2)}) collective-permute-start(bf16[96,96]{1,0:T(8,128)(2,1)S(1)} %get-tuple-element.23), channel_id=1, source_target_pairs={{0,8},{4,12},{8,0},{12,4},{1,9},{5,13},{9,1},{13,5},{2,10},{6,14},... | collective-permute-start | bytes 55304 | tf_op jit(solution)/shard_map/ppermute | solution.py:415
  40.9 3.3 %collective-permute-start.11 = (bf16[96,96]{1,0:T(8,128)(2,1)S(1)}, bf16[96,96]{1,0:T(8,128)(2,1)S(1)}, u32[]{:S(2)}, u32[]{:S(2)}) collective-permute-start(bf16[96,96]{1,0:T(8,128)(2,1)S(1)} %get-tuple-element.24), channel_id=1, source_target_pairs={{0,12},{4,8},{8,4},{12,0},{1,13},{5,9},{9,5},{13,1},{2,14},{6,10},... | collective-permute-start | bytes 55304 | tf_op jit(solution)/shard_map/ppermute | solution.py:415
  44.3 7.0 %collective-permute-start.14 = (bf16[96,384]{1,0:T(8,128)(2,1)S(1)}, bf16[96,384]{1,0:T(8,128)(2,1)S(1)}, u32[]{:S(2)}, u32[]{:S(2)}) collective-permute-start(bf16[96,384]{1,0:T(8,128)(2,1)S(1)} %shard_map.155.own_ref), channel_id=1, source_target_pairs={{0,3},{1,2},{2,1},{3,0},{4,7},{5,6},{6,5},{7,4},{8,11},{9,10},{10,... | collective-permute-start | bytes 221192 | tf_op jit(solution)/shard_map/ppermute | solution.py:415
  47.8 5.9 %collective-permute-start.13 = (bf16[96,384]{1,0:T(8,128)(2,1)S(1)}, bf16[96,384]{1,0:T(8,128)(2,1)S(1)}, u32[]{:S(2)}, u32[]{:S(2)}) collective-permute-start(bf16[96,384]{1,0:T(8,128)(2,1)S(1)} %shard_map.155.own_ref), channel_id=1, source_target_pairs={{0,2},{1,3},{2,0},{3,1},{4,6},{5,7},{6,4},{7,5},{8,10},{9,11},{10,... | collective-permute-start | bytes 221192 | tf_op jit(solution)/shard_map/ppermute | solution.py:415
  47.8 6.2 %collective-permute-start.12 = (bf16[96,384]{1,0:T(8,128)(2,1)S(1)}, bf16[96,384]{1,0:T(8,128)(2,1)S(1)}, u32[]{:S(2)}, u32[]{:S(2)}) collective-permute-start(bf16[96,384]{1,0:T(8,128)(2,1)S(1)} %shard_map.155.own_ref), channel_id=1, source_target_pairs={{0,1},{1,0},{2,3},{3,2},{4,5},{5,4},{6,7},{7,6},{8,9},{9,8},{10,11... | collective-permute-start | bytes 221192 | tf_op jit(solution)/shard_map/ppermute | solution.py:415
